TPU v7x, 32 devices: a whole 2x2x4 slice. The times are simulated.
32 devices in a mesh: ctx: 16 (over z, y, core), wt: 2 (over x).
Axes of the slice: x: 2, y: 2, z: 4, core: 2. Of those that a mesh axis runs over, the one named last changes fastest.
Arguments:
- tokens: bfloat16 [2, 2048, 1024], P('wt', 'ctx'), may hold values from -6 to 6
- cotangent: bfloat16 [2, 2048, 1024], P('wt', 'ctx'), may hold values from -6 to 6
- pair_order: int32 [16], replicated, may hold values from 0 to 15, each once
- norm_gains: float32 [2, 1024], replicated, may hold values from 0.5 to 1.5
- head_gains: float32 [2, 128], replicated, may hold values from 1 to 1.7
- gate_head: bfloat16 [16, 1024], replicated, may hold values from -0.1875 to 0.1875
- w_query: bfloat16 [2048, 1024], P('wt'), may hold values from -0.1875 to 0.1875
- w_keyval: bfloat16 [2, 1024, 1024], P(None, 'wt'), may hold values from -0.1875 to 0.1875
- w_outproj: bfloat16 [2048, 1024], P('wt'), may hold values from -2 to 2
- w_gateup: bfloat16 [2, 3072, 1024], P(None, 'wt'), may hold values from -0.1875 to 0.1875
- w_down: bfloat16 [3072, 1024], P('wt'), may hold values from -0.109375 to 0.109375
- mom_norm: float32 [2, 1024], replicated
- mom_head: float32 [2, 128], replicated
- mom_gate_head: float32 [16, 1024], replicated
- mom_query: float32 [2048, 1024], P(('ctx', 'wt'))
- mom_keyval: float32 [2, 1024, 1024], P(None, ('ctx', 'wt'))
- mom_outproj: float32 [2048, 1024], P(('ctx', 'wt'))
- mom_gateup: float32 [2, 3072, 1024], P(None, ('ctx', 'wt'))
- mom_down: float32 [3072, 1024], P(('ctx', 'wt'))
Outputs:
- output: bfloat16 [2, 2048, 1024], P('wt', 'ctx')
- grad_input: float32 [2, 2048, 1024], P('wt', 'ctx')
- grad_norm_gains: float32 [2, 1024], replicated
- grad_head_gains: float32 [2, 128], replicated
- grad_gate_head: float32 [16, 1024], replicated
- grad_query: float32 [2048, 1024], P(('ctx', 'wt'))
- grad_keyval: float32 [2, 1024, 1024], P(None, ('ctx', 'wt'))
- grad_outproj: float32 [2048, 1024], P(('ctx', 'wt'))
- grad_gateup: float32 [2, 3072, 1024], P(None, ('ctx', 'wt'))
- grad_down: float32 [3072, 1024], P(('ctx', 'wt'))
- new_mom_norm: float32 [2, 1024], replicated
- new_mom_head: float32 [2, 128], replicated
- new_mom_gate_head: float32 [16, 1024], replicated
- new_mom_query: float32 [2048, 1024], P(('ctx', 'wt'))
- new_mom_keyval: float32 [2, 1024, 1024], P(None, ('ctx', 'wt'))
- new_mom_outproj: float32 [2048, 1024], P(('ctx', 'wt'))
- new_mom_gateup: float32 [2, 3072, 1024], P(None, ('ctx', 'wt'))
- new_mom_down: float32 [3072, 1024], P(('ctx', 'wt'))
- new_norm_gains: float32 [2, 1024], replicated
- new_head_gains: float32 [2, 128], replicated
- new_gate_head: float32 [16, 1024], replicated
- new_query: float32 [2048, 1024], P(('ctx', 'wt'))
- new_keyval: float32 [2, 1024, 1024], P(None, ('ctx', 'wt'))
- new_outproj: float32 [2048, 1024], P(('ctx', 'wt'))
- new_gateup: float32 [2, 3072, 1024], P(None, ('ctx', 'wt'))
- new_down: float32 [3072, 1024], P(('ctx', 'wt'))
Inputs may be any that keep to these rules, and one draw needn't show every extreme that they name: The rows of stored block i of 128 rows hold, first, the positions of block pair_order[i] of 64 positions and then those of block 31 - pair_order[i]; each value appears once.
All inputs are finite; a program needn't handle non-finite values.
Results may differ from a plain program's by a relative error of at most 0.022.
Values may be sent and summed in bfloat16 or wider, within the bound.
No kernel may reach another device: no remote copies, remote signals or barrier semaphores. Data moves between devices by JAX's collectives and lax.ppermute only.
A program may use at most 384 MiB of HBM per device.

v0:
```python
import math

import jax
import jax.numpy as jnp
from jax import lax
from jax.sharding import PartitionSpec as P

NS_STEPS = 5


HIGH_PRECISION = lax.Precision.HIGHEST
NORM_EPS = 1e-06
ROPE_BASE = 1000000.0
SCHULZ_FIRST = 3.4445
SCHULZ_SECOND = -4.775
SCHULZ_THIRD = 2.0315
MOMENT_DECAY = 0.5
MATRIX_RATE = 0.03
VECTOR_RATE = 0.003


def positions(first_row, rows_in, pair_order, tok_dev):
    row_ids = first_row + jnp.arange(rows_in, dtype=jnp.int32)
    device_ids = row_ids // tok_dev
    offsets = row_ids % tok_dev
    piece_len = tok_dev // 2
    cycle_ids = jnp.arange(pair_order.shape[0], dtype=jnp.int32)
    owned = jnp.sum(
        jnp.where(device_ids[:, None] == cycle_ids[None, :], pair_order[None, :], 0), axis=1
    )
    block_ids = jnp.where(offsets < piece_len, owned, 2 * pair_order.shape[0] - 1 - owned)
    return block_ids * piece_len + offsets % piece_len


def rope_tables(token_place, head_dim):
    half_dim = head_dim // 2
    inverse = ROPE_BASE ** (-(2.0 * jnp.arange(half_dim, dtype=jnp.float32)) / head_dim)
    angles = token_place.astype(jnp.float32)[:, None] * inverse[None, :]
    return (jnp.cos(angles)[:, None, :], jnp.sin(angles)[:, None, :])


def rotate(values_in, cosine, sine_part):
    half_dim = values_in.shape[-1] // 2
    leading = values_in[..., :half_dim]
    trailing = values_in[..., half_dim:]
    return jnp.concatenate(
        [leading * cosine - trailing * sine_part, trailing * cosine + leading * sine_part], axis=-1
    )


def rotate_back(grads_in, cosine, sine_part):
    half_dim = grads_in.shape[-1] // 2
    leading = grads_in[..., :half_dim]
    trailing = grads_in[..., half_dim:]
    return jnp.concatenate(
        [leading * cosine + trailing * sine_part, trailing * cosine - leading * sine_part], axis=-1
    )


def rms_scale(values_in):
    return lax.rsqrt(jnp.mean(values_in * values_in, axis=-1, keepdims=True) + NORM_EPS)


def norm_back(grad_out, scaled, rscale, gains):
    pushed = grad_out * gains
    grad_in = rscale * (pushed - scaled * jnp.mean(pushed * scaled, axis=-1, keepdims=True))
    return (grad_in, grad_out * scaled)


def project(acts, weight):
    return lax.dot_general(
        acts, weight, (((1,), (1,)), ((), ())), preferred_element_type=jnp.float32
    )


def outer(grad_rows, act_rows):
    return lax.dot_general(
        grad_rows, act_rows, (((0,), (0,)), ((), ())), preferred_element_type=jnp.float32
    )


def block_weights(query_part, key_part, query_place, key_place, scale_factor):
    raw_scores = jnp.einsum(
        "qkgd,nkd->kgqn", query_part, key_part, preferred_element_type=jnp.float32
    )
    allowed = key_place[None, None, None, :] <= query_place[None, None, :, None]
    return jnp.where(allowed, jnp.exp(raw_scores * scale_factor), 0.0)


def fold_blocks(update, totals, pieces):
    rows_in = pieces[0].shape[0]
    block_len = 512
    blocked = tuple(
        (member.reshape((rows_in // block_len, block_len) + member.shape[1:]) for member in pieces)
    )
    starts = block_len * jnp.arange(rows_in // block_len, dtype=jnp.int32)

    def scan_step(running, inside):
        return (update(running, inside[0], inside[1]), None)

    result, unused = lax.scan(scan_step, totals, (blocked, starts))
    return result


def schulz_step(current, gram_full):
    product = jnp.einsum("krd,kde->kre", current, gram_full, precision=HIGH_PRECISION)
    return (
        SCHULZ_FIRST * current
        + SCHULZ_SECOND * product
        + SCHULZ_THIRD * jnp.einsum("krd,kde->kre", product, gram_full, precision=HIGH_PRECISION)
    )


def on_device(
    tokens,
    cotangent,
    pair_order,
    norm_gains,
    head_gains,
    gate_head,
    w_query,
    w_keyval,
    w_outproj,
    w_gateup,
    w_down,
    mom_norm,
    mom_head,
    mom_gate_head,
    mom_query,
    mom_keyval,
    mom_outproj,
    mom_gateup,
    mom_down,
):
    cycle_len = lax.axis_size("ctx")
    pair_len = lax.axis_size("wt")
    inputs = tokens[0].astype(jnp.float32)
    tok_dev = inputs.shape[0]
    head_count = gate_head.shape[0]
    head_dim = head_gains.shape[1]
    kv_count = w_keyval.shape[1] * pair_len // head_dim
    group_len = head_count // kv_count
    scale_factor = 1.0 / math.sqrt(head_dim)
    token_place = positions(lax.axis_index("ctx") * tok_dev, tok_dev, pair_order, tok_dev)
    cosine, sine_part = rope_tables(token_place, head_dim)
    full_query, full_keyval, full_outproj = (
        lax.all_gather(w_query, "wt", axis=0, tiled=True),
        lax.all_gather(w_keyval, "wt", axis=1, tiled=True),
        lax.all_gather(w_outproj, "wt", axis=0, tiled=True),
    )
    rscale_in = rms_scale(inputs)
    scaled_in = inputs * rscale_in
    normed = (scaled_in * norm_gains[0]).astype(jnp.bfloat16)
    query_raw = project(normed, full_query).reshape(tok_dev, head_count, head_dim)
    key_raw = project(normed, full_keyval[0]).reshape(tok_dev, kv_count, head_dim)
    value_rows = (
        project(normed, full_keyval[1]).astype(jnp.bfloat16).reshape(tok_dev, kv_count, head_dim)
    )
    gate_logit = project(normed, gate_head)
    rscale_query = rms_scale(query_raw)
    scaled_query = query_raw * rscale_query
    query_rows = rotate(scaled_query * head_gains[0], cosine, sine_part).astype(jnp.bfloat16)
    rscale_key = rms_scale(key_raw)
    scaled_key = key_raw * rscale_key
    key_rows = rotate(scaled_key * head_gains[1], cosine, sine_part).astype(jnp.bfloat16)
    query_grouped = query_rows.reshape(tok_dev, kv_count, group_len, head_dim)

    def forward_update(totals, pieces, first_row):
        key_piece, value_piece = pieces
        key_place = positions(first_row, key_piece.shape[0], pair_order, tok_dev)
        weights = block_weights(query_grouped, key_piece, token_place, key_place, scale_factor)
        weighted_sum = totals[0] + jnp.einsum(
            "kgqn,nkd->qkgd",
            weights.astype(jnp.bfloat16),
            value_piece,
            preferred_element_type=jnp.float32,
        )
        return (weighted_sum, totals[1] + jnp.sum(weights, axis=-1))

    start_sum = jnp.zeros((tok_dev, kv_count, group_len, head_dim), jnp.float32)
    start_total = jnp.zeros((kv_count, group_len, tok_dev), jnp.float32)
    weighted_sum, weight_total = fold_blocks(
        forward_update,
        (start_sum, start_total),
        (
            lax.all_gather(key_rows, "ctx", axis=0, tiled=True),
            lax.all_gather(value_rows, "ctx", axis=0, tiled=True),
        ),
    )
    total_rows = jnp.transpose(weight_total, (2, 0, 1))
    attended_grouped = weighted_sum / total_rows[..., None]
    attended = attended_grouped.reshape(tok_dev, head_count, head_dim)
    gate_sig = jax.nn.sigmoid(gate_logit)
    gated_rows = (
        (attended * gate_sig[:, :, None])
        .reshape(tok_dev, head_count * head_dim)
        .astype(jnp.bfloat16)
    )
    middle = inputs + jnp.dot(gated_rows, full_outproj, preferred_element_type=jnp.float32)
    full_gateup, full_down = (
        lax.all_gather(w_gateup, "wt", axis=1, tiled=True),
        lax.all_gather(w_down, "wt", axis=0, tiled=True),
    )
    rscale_mid = rms_scale(middle)
    scaled_mid = middle * rscale_mid
    hidden_in = (scaled_mid * norm_gains[1]).astype(jnp.bfloat16)
    gate_part = project(hidden_in, full_gateup[0])
    up_part = project(hidden_in, full_gateup[1])
    gate_sigmoid = jax.nn.sigmoid(gate_part)
    silu_part = gate_part * gate_sigmoid
    hidden = (silu_part * up_part).astype(jnp.bfloat16)
    output = (middle + jnp.dot(hidden, full_down, preferred_element_type=jnp.float32)).astype(
        jnp.bfloat16
    )
    grad_out = cotangent[0].astype(jnp.float32)
    grad_out_low = grad_out.astype(jnp.bfloat16)
    grad_down = outer(hidden, grad_out_low)
    dhidden = project(grad_out_low, full_down)
    dgate_low = (
        dhidden * up_part * gate_sigmoid * (1.0 + gate_part * (1.0 - gate_sigmoid))
    ).astype(jnp.bfloat16)
    dup_low = (dhidden * silu_part).astype(jnp.bfloat16)
    grad_gateup = jnp.stack([outer(dgate_low, hidden_in), outer(dup_low, hidden_in)])
    dhidden_in = jnp.dot(dgate_low, full_gateup[0], preferred_element_type=jnp.float32) + jnp.dot(
        dup_low, full_gateup[1], preferred_element_type=jnp.float32
    )
    dmiddle_norm, gain_mid_terms = norm_back(dhidden_in, scaled_mid, rscale_mid, norm_gains[1])
    dmiddle = grad_out + dmiddle_norm
    dbranch = dmiddle.astype(jnp.bfloat16)
    grad_outproj = outer(gated_rows, dbranch)
    dgated = project(dbranch, full_outproj).reshape(tok_dev, head_count, head_dim)
    dattended = dgated * gate_sig[:, :, None]
    dgate_logit = (jnp.sum(dgated * attended, axis=-1) * gate_sig * (1.0 - gate_sig)).astype(
        jnp.bfloat16
    )
    dattended_grouped = dattended.reshape(tok_dev, kv_count, group_len, head_dim)
    back_weighted = (dattended_grouped / total_rows[..., None]).astype(jnp.bfloat16)
    correction = jnp.sum(dattended_grouped * attended_grouped, axis=-1) / total_rows
    local_correction = jnp.transpose(correction, (1, 2, 0))

    def query_update(totals, pieces, first_row):
        key_piece, value_piece = pieces
        key_place = positions(first_row, key_piece.shape[0], pair_order, tok_dev)
        weights = block_weights(query_grouped, key_piece, token_place, key_place, scale_factor)
        pushed = jnp.einsum(
            "qkgd,nkd->kgqn", back_weighted, value_piece, preferred_element_type=jnp.float32
        )
        score_grad = (scale_factor * weights * (pushed - local_correction[..., None])).astype(
            jnp.bfloat16
        )
        return totals + jnp.einsum(
            "kgqn,nkd->qkgd", score_grad, key_piece, preferred_element_type=jnp.float32
        )

    dquery = fold_blocks(
        query_update,
        jnp.zeros((tok_dev, kv_count, group_len, head_dim), jnp.float32),
        (
            lax.all_gather(key_rows, "ctx", axis=0, tiled=True),
            lax.all_gather(value_rows, "ctx", axis=0, tiled=True),
        ),
    )

    def key_update(totals, pieces, first_row):
        far_query, far_back, far_correction = pieces
        query_place = positions(first_row, far_query.shape[0], pair_order, tok_dev)
        weights = block_weights(far_query, key_rows, query_place, token_place, scale_factor)
        pushed = jnp.einsum(
            "qkgd,nkd->kgqn", far_back, value_rows, preferred_element_type=jnp.float32
        )
        score_grad = (
            scale_factor * weights * (pushed - jnp.transpose(far_correction, (1, 2, 0))[..., None])
        ).astype(jnp.bfloat16)
        key_grad = totals[0] + jnp.einsum(
            "kgqn,qkgd->nkd", score_grad, far_query, preferred_element_type=jnp.float32
        )
        value_grad = totals[1] + jnp.einsum(
            "kgqn,qkgd->nkd",
            weights.astype(jnp.bfloat16),
            far_back,
            preferred_element_type=jnp.float32,
        )
        return (key_grad, value_grad)

    start_keys = jnp.zeros((tok_dev, kv_count, head_dim), jnp.float32)
    dkey, dvalue = fold_blocks(
        key_update,
        (start_keys, start_keys),
        (
            lax.all_gather(query_grouped, "ctx", axis=0, tiled=True),
            lax.all_gather(back_weighted, "ctx", axis=0, tiled=True),
            lax.all_gather(correction.astype(jnp.bfloat16), "ctx", axis=0, tiled=True).astype(
                jnp.float32
            ),
        ),
    )
    dquery_norm = rotate_back(dquery.reshape(tok_dev, head_count, head_dim), cosine, sine_part)
    dq_raw, head_query_terms = norm_back(dquery_norm, scaled_query, rscale_query, head_gains[0])
    dkey_norm = rotate_back(dkey, cosine, sine_part)
    dk_raw, head_key_terms = norm_back(dkey_norm, scaled_key, rscale_key, head_gains[1])
    dq_low = dq_raw.reshape(tok_dev, head_count * head_dim).astype(jnp.bfloat16)
    dk_low = dk_raw.reshape(tok_dev, kv_count * head_dim).astype(jnp.bfloat16)
    dv_low = dvalue.reshape(tok_dev, kv_count * head_dim).astype(jnp.bfloat16)
    grad_query = outer(dq_low, normed)
    grad_keyval = jnp.stack([outer(dk_low, normed), outer(dv_low, normed)])
    grad_gate_head = outer(dgate_logit, normed)
    dnormed = (
        jnp.dot(dq_low, full_query, preferred_element_type=jnp.float32)
        + jnp.dot(dk_low, full_keyval[0], preferred_element_type=jnp.float32)
        + jnp.dot(dv_low, full_keyval[1], preferred_element_type=jnp.float32)
        + jnp.dot(dgate_logit, gate_head, preferred_element_type=jnp.float32)
    )
    dinput_norm, gain_in_terms = norm_back(dnormed, scaled_in, rscale_in, norm_gains[0])
    grad_input = dmiddle + dinput_norm
    shard_query, shard_keyval, shard_outproj, shard_gateup, shard_down = (
        lax.psum_scatter(grad_query, ("ctx", "wt"), scatter_dimension=0, tiled=True),
        lax.psum_scatter(grad_keyval, ("ctx", "wt"), scatter_dimension=1, tiled=True),
        lax.psum_scatter(grad_outproj, ("ctx", "wt"), scatter_dimension=0, tiled=True),
        lax.psum_scatter(grad_gateup, ("ctx", "wt"), scatter_dimension=1, tiled=True),
        lax.psum_scatter(grad_down, ("ctx", "wt"), scatter_dimension=0, tiled=True),
    )
    norm_terms = jnp.stack([jnp.sum(gain_in_terms, axis=0), jnp.sum(gain_mid_terms, axis=0)])
    head_terms = jnp.stack(
        [jnp.sum(head_query_terms, axis=(0, 1)), jnp.sum(head_key_terms, axis=(0, 1))]
    )
    grad_norm_gains, grad_head_gains, grad_gate_sum = lax.psum(
        (norm_terms, head_terms, grad_gate_head), ("ctx", "wt")
    )
    new_mom_norm = MOMENT_DECAY * mom_norm + (1.0 - MOMENT_DECAY) * grad_norm_gains
    new_mom_head = MOMENT_DECAY * mom_head + (1.0 - MOMENT_DECAY) * grad_head_gains
    new_mom_gate = MOMENT_DECAY * mom_gate_head + (1.0 - MOMENT_DECAY) * grad_gate_sum
    new_norm = norm_gains - VECTOR_RATE * new_mom_norm
    new_head = head_gains - VECTOR_RATE * new_mom_head
    new_gate = gate_head.astype(jnp.float32) - VECTOR_RATE * new_mom_gate
    grad_list = [
        shard_query,
        shard_keyval[0],
        shard_keyval[1],
        shard_outproj,
        shard_gateup[0],
        shard_gateup[1],
        shard_down,
    ]
    moment_list = [
        mom_query,
        mom_keyval[0],
        mom_keyval[1],
        mom_outproj,
        mom_gateup[0],
        mom_gateup[1],
        mom_down,
    ]
    full_list = [
        full_query,
        full_keyval[0],
        full_keyval[1],
        full_outproj,
        full_gateup[0],
        full_gateup[1],
        full_down,
    ]
    new_moments = [
        MOMENT_DECAY * moment + (1.0 - MOMENT_DECAY) * gradient
        for moment, gradient in zip(moment_list, grad_list)
    ]
    squares = lax.psum(
        jnp.stack([jnp.sum(moment * moment) for moment in new_moments]), ("ctx", "wt")
    )
    norm_roots = jnp.sqrt(squares) + 1e-07
    first_set = [0, 3, 1, 2]
    second_set = [4, 5, 6]
    pad_rows = max((moment.shape[0] for moment in new_moments))
    width_all = new_moments[0].shape[1]

    def padded(member):
        matrix = new_moments[member]
        return jnp.pad(matrix, ((0, pad_rows - matrix.shape[0]), (0, 0)))

    blank_rows = jnp.zeros((pad_rows, width_all), jnp.float32)
    outgoing = jnp.stack(
        [
            jnp.stack([padded(member) for member in first_set]),
            jnp.stack([padded(member) for member in second_set] + [blank_rows]),
        ]
    )
    incoming = lax.all_to_all(
        outgoing.astype(jnp.bfloat16), "wt", split_axis=0, concat_axis=0, tiled=True
    ).astype(outgoing.dtype)
    group_rows = jnp.concatenate([incoming[0], incoming[1]], axis=1)
    first_roots = jnp.stack([norm_roots[member] for member in first_set])
    second_roots = jnp.stack(
        [norm_roots[member] for member in second_set] + [jnp.ones((), jnp.float32)]
    )
    group_roots = jnp.where(lax.axis_index("wt") == 0, first_roots, second_roots)
    group_now = group_rows / group_roots[:, None, None]
    for sweep in range(NS_STEPS):
        partial_gram = jnp.einsum("krd,kre->kde", group_now, group_now, precision=HIGH_PRECISION)
        gram_part = lax.psum_scatter(partial_gram, "ctx", scatter_dimension=1, tiled=True)
        gram_full = lax.all_gather(
            gram_part.astype(jnp.bfloat16), "ctx", axis=1, tiled=True
        ).astype(gram_part.dtype)
        group_now = schulz_step(group_now, gram_full)
    leaving = jnp.stack([group_now[:, :pad_rows], group_now[:, pad_rows:]])
    returned = lax.all_to_all(
        leaving.astype(jnp.bfloat16), "wt", split_axis=0, concat_axis=0, tiled=True
    ).astype(leaving.dtype)
    current = [None] * len(new_moments)
    for slot_id, member in enumerate(first_set):
        current[member] = returned[0, slot_id, : new_moments[member].shape[0]]
    for slot_id, member in enumerate(second_set):
        current[member] = returned[1, slot_id, : new_moments[member].shape[0]]
    block_id = lax.axis_index("ctx") * pair_len + lax.axis_index("wt")
    seq_len = tok_dev * cycle_len
    new_weights = []
    for member in range(len(current)):
        full_rows = full_list[member].shape[0]
        width_cols = full_list[member].shape[1]
        boost = math.sqrt(width_cols / max(1, 16384 // seq_len)) if member == 3 else 1.0
        rows_each = full_rows // (cycle_len * pair_len)
        old_rows = lax.dynamic_slice_in_dim(
            full_list[member], block_id * rows_each, rows_each, 0
        ).astype(jnp.float32)
        new_weights.append(old_rows - boost * MATRIX_RATE * math.sqrt(full_rows) * current[member])
    return (
        output[None],
        grad_input[None],
        grad_norm_gains,
        grad_head_gains,
        grad_gate_sum,
        shard_query,
        shard_keyval,
        shard_outproj,
        shard_gateup,
        shard_down,
        new_mom_norm,
        new_mom_head,
        new_mom_gate,
        new_moments[0],
        jnp.stack([new_moments[1], new_moments[2]]),
        new_moments[3],
        jnp.stack([new_moments[4], new_moments[5]]),
        new_moments[6],
        new_norm,
        new_head,
        new_gate,
        new_weights[0],
        jnp.stack([new_weights[1], new_weights[2]]),
        new_weights[3],
        jnp.stack([new_weights[4], new_weights[5]]),
        new_weights[6],
    )


def solution(mesh):
    placed = (
        P("wt", "ctx", None),
        P("wt", "ctx", None),
        P(),
        P(),
        P(),
        P(),
        P("wt", None),
        P(None, "wt", None),
        P("wt", None),
        P(None, "wt", None),
        P("wt", None),
        P(),
        P(),
        P(),
        P(("ctx", "wt"), None),
        P(None, ("ctx", "wt"), None),
        P(("ctx", "wt"), None),
        P(None, ("ctx", "wt"), None),
        P(("ctx", "wt"), None),
    )
    return jax.shard_map(
        on_device,
        mesh=mesh,
        in_specs=placed,
        out_specs=(
            P("wt", "ctx", None),
            P("wt", "ctx", None),
            P(),
            P(),
            P(),
            P(("ctx", "wt"), None),
            P(None, ("ctx", "wt"), None),
            P(("ctx", "wt"), None),
            P(None, ("ctx", "wt"), None),
            P(("ctx", "wt"), None),
            P(),
            P(),
            P(),
            P(("ctx", "wt"), None),
            P(None, ("ctx", "wt"), None),
            P(("ctx", "wt"), None),
            P(None, ("ctx", "wt"), None),
            P(("ctx", "wt"), None),
            P(),
            P(),
            P(),
            P(("ctx", "wt"), None),
            P(None, ("ctx", "wt"), None),
            P(("ctx", "wt"), None),
            P(None, ("ctx", "wt"), None),
            P(("ctx", "wt"), None),
        ),
        check_vma=False,
    )
```

profile of v0, /device:TPU:0, one launch (start us, length us, event | category | flops | bytes accessed | tf_op | source)
XLA Modules:
  0.0 3328.0 jit_solution(4623426215725593024)
XLA Ops:
  11.3 57.7 %all-gather.15.cloned.1.call-done = bf16[2,1024,1024]{2,1,0:T(8,128)(2,1)} async-done(((bf16[2,512,1024]{2,1,0:T(8,128)(2,1)}), bf16[2,1024,1024]{2,1,0:T(8,128)(2,1)}) %all-gather.15.cloned.1.call-update) | async-done | bytes 4194320 | tf_op jit(solution)/shard_map/all_gather | solution.py:148
  134.5 74.9 %all-gather.27.cloned.1.call-done = bf16[3072,1024]{1,0:T(8,128)(2,1)} async-done(((bf16[1536,1024]{1,0:T(8,128)(2,1)}), bf16[3072,1024]{1,0:T(8,128)(2,1)}) %all-gather.27.cloned.1.call-update) | async-done | bytes 6291472 | tf_op jit(solution)/shard_map/all_gather | solution.py:202
  215.5 49.7 %all-gather.19.cloned.1.call-done = bf16[2048,8,128]{0,2,1:T(8,128)(2,1)} async-done(((bf16[128,8,128]{0,2,1:T(8,128)(2,1)}), bf16[2048,8,128]{0,2,1:T(8,128)(2,1)}) %all-gather.19.cloned.1.call-update) | async-done | bytes 4194320 | tf_op jit(solution)/shard_map/all_gather | solution.py:186
  316.5 54.6 %while.46 = (s32[]{:T(128)}, f32[128,8,2,128]{0,3,2,1:T(8,128)S(1)}, f32[8,2,128]{2,1,0:T(2,128)S(1)}, bf16[4,512,8,128]{3,2,1,0:T(8,128)(2,1)}, s32[4]{0:T(128)...) while((s32[]{:T(128)}, ...), condition=%wide.region_7.8_spmd.clone, body=%wide.region_4.7_spmd.clone.sunk | while | flops 543800832 | bytes 17576696 | solution.py:101
  376.5 149.8 %all-gather.25.cloned.1.call-done = bf16[2,3072,1024]{2,1,0:T(8,128)(2,1)} async-done(((bf16[2,1536,1024]{2,1,0:T(8,128)(2,1)}), bf16[2,3072,1024]{2,1,0:T(8,128)(2,1)}) %all-gather.25.cloned.1.call-update) | async-done | bytes 12582928 | tf_op jit(solution)/shard_map/all_gather | solution.py:201
  548.7 57.1 %while.47 = (s32[]{:T(128)}, f32[128,8,2,128]{0,3,2,1:T(8,128)}, bf16[4,512,8,128]{3,1,2,0:T(8,128)(2,1)}, s32[4]{0:T(128)}, s32[16]{0:T(128)}, /*index=5*/s32[1...) while((s32[]{:T(128)}, f32[128,8,2,128]{0,3,2,1:T(8,128)}, ...), condition=%wide.region_13.14_spmd.clone, body=%wide.region_11.13_spmd.clone.sunk | while | flops 812234240 | bytes 16929512 | solution.py:101
  700.3 92.4 %while.48 = (s32[]{:T(128)}, f32[128,8,128]{0,2,1:T(8,128)}, f32[128,8,128]{0,2,1:T(8,128)}, bf16[4,512,8,2,128]{4,2,3,1,0:T(8,128)(2,1)}, s32[128]{0:T(128)S(1)...) while((s32[]{:T(128)}, f32[128,8,128]{0,2,1:T(8,128)}, ...), condition=%wide.region_17.18_spmd.clone, body=%wide.region_15.17_spmd.clone.sunk | while | flops 1083815424 | bytes 32355052 | solution.py:101
  825.4 59.0 %reduce-scatter.11.cloned.1.call-done = f32[64,1024]{1,0:T(8,128)} async-done(((f32[2048,1024]{1,0:T(8,128)}), f32[64,1024]{1,0:T(8,128)}) %reduce-scatter.11.cloned.1.call-update) | async-done | bytes 262160 | tf_op jit(solution)/shard_map/reduce_scatter | solution.py:316
  886.8 184.5 %reduce-scatter.15.cloned.1.call-done = f32[64,1024]{1,0:T(8,128)} async-done(((f32[2048,1024]{1,0:T(8,128)}), f32[64,1024]{1,0:T(8,128)}) %reduce-scatter.15.cloned.1.call-update) | async-done | bytes 262160 | tf_op jit(solution)/shard_map/reduce_scatter | solution.py:318
  1073.0 161.1 %reduce-scatter.19.cloned.1.call-done = f32[96,1024]{1,0:T(8,128)} async-done(((f32[3072,1024]{1,0:T(8,128)}), f32[96,1024]{1,0:T(8,128)}) %reduce-scatter.19.cloned.1.call-update) | async-done | bytes 393232 | tf_op jit(solution)/shard_map/reduce_scatter | solution.py:320
  1237.3 182.1 %reduce-scatter.13.cloned.1.call-done = f32[2,32,1024]{2,1,0:T(8,128)} async-done(((f32[2,1024,1024]{2,1,0:T(8,128)}), f32[2,32,1024]{2,1,0:T(8,128)}) %reduce-scatter.13.cloned.1.call-update) | async-done | bytes 262160 | tf_op jit(solution)/shard_map/reduce_scatter | solution.py:317
  1421.1 252.5 %reduce-scatter.17.cloned.1.call-done = f32[2,96,1024]{2,1,0:T(8,128)} async-done(((f32[2,3072,1024]{2,1,0:T(8,128)}), f32[2,96,1024]{2,1,0:T(8,128)}) %reduce-scatter.17.cloned.1.call-update) | async-done | bytes 786448 | tf_op jit(solution)/shard_map/reduce_scatter | solution.py:319
  1688.2 45.7 %all-reduce.4 = (f32[2,1024]{1,0:T(2,128)}, f32[2,128]{1,0:T(2,128)}, f32[7]{0:T(128)S(1)}) all-reduce(f32[2,1024]{1,0:T(2,128)S(1)} %pad_maximum_fusion.12, f32[2,128]{1,0:T(2,128)S(1)} %pad_maximum_fusion.13, f32[7]{0:T(128)S(1)} %stack.173), channel_id=1, replica_groups=mesh['ctx'=16,'wt'=2] {'ctx','wt'}, use_global_device_ids=true, to_apply=%region_23.24 | all-reduce | flops 2311 | bytes 18488 | tf_op jit(solution)/shard_map/psum | solution.py:326
  1753.4 178.1 %reduce-scatter.21.cloned.1.call-done = f32[4,64,1024]{2,1,0:T(8,128)} async-done(((f32[4,1024,1024]{2,1,0:T(8,128)}), f32[4,64,1024]{2,1,0:T(8,128)}) %reduce-scatter.21.cloned.1.call-update) | async-done | bytes 1048592 | tf_op jit(solution)/shard_map/reduce_scatter | solution.py:398
  1933.8 74.2 %all-gather.33.cloned.1.call-done = bf16[4,1024,1024]{2,1,0:T(8,128)(2,1)} async-done(((bf16[4,64,1024]{2,1,0:T(8,128)(2,1)}), bf16[4,1024,1024]{2,1,0:T(8,128)(2,1)}) %all-gather.33.cloned.1.call-update) | async-done | bytes 8388624 | tf_op jit(solution)/shard_map/all_gather | solution.py:399
  2039.7 176.9 %reduce-scatter.23.cloned.1.call-done = f32[4,64,1024]{2,1,0:T(8,128)} async-done(((f32[4,1024,1024]{2,1,0:T(8,128)}), f32[4,64,1024]{2,1,0:T(8,128)}) %reduce-scatter.23.cloned.1.call-update) | async-done | bytes 1048592 | tf_op jit(solution)/shard_map/reduce_scatter | solution.py:398
  2219.2 74.0 %all-gather.35.cloned.1.call-done = bf16[4,1024,1024]{2,1,0:T(8,128)(2,1)} async-done(((bf16[4,64,1024]{2,1,0:T(8,128)(2,1)}), bf16[4,1024,1024]{2,1,0:T(8,128)(2,1)}) %all-gather.35.cloned.1.call-update) | async-done | bytes 8388624 | tf_op jit(solution)/shard_map/all_gather | solution.py:399
  2325.5 176.9 %reduce-scatter.25.cloned.1.call-done = f32[4,64,1024]{2,1,0:T(8,128)} async-done(((f32[4,1024,1024]{2,1,0:T(8,128)}), f32[4,64,1024]{2,1,0:T(8,128)}) %reduce-scatter.25.cloned.1.call-update) | async-done | bytes 1048592 | tf_op jit(solution)/shard_map/reduce_scatter | solution.py:398
  2504.8 74.2 %all-gather.37.cloned.1.call-done = bf16[4,1024,1024]{2,1,0:T(8,128)(2,1)} async-done(((bf16[4,64,1024]{2,1,0:T(8,128)(2,1)}), bf16[4,1024,1024]{2,1,0:T(8,128)(2,1)}) %all-gather.37.cloned.1.call-update) | async-done | bytes 8388624 | tf_op jit(solution)/shard_map/all_gather | solution.py:399
  2611.5 176.9 %reduce-scatter.27.cloned.1.call-done = f32[4,64,1024]{2,1,0:T(8,128)} async-done(((f32[4,1024,1024]{2,1,0:T(8,128)}), f32[4,64,1024]{2,1,0:T(8,128)}) %reduce-scatter.27.cloned.1.call-update) | async-done | bytes 1048592 | tf_op jit(solution)/shard_map/reduce_scatter | solution.py:398
  2790.8 74.4 %all-gather.39.cloned.1.call-done = bf16[4,1024,1024]{2,1,0:T(8,128)(2,1)} async-done(((bf16[4,64,1024]{2,1,0:T(8,128)(2,1)}), bf16[4,1024,1024]{2,1,0:T(8,128)(2,1)}) %all-gather.39.cloned.1.call-update) | async-done | bytes 8388624 | tf_op jit(solution)/shard_map/all_gather | solution.py:399
  2896.5 175.4 %reduce-scatter.29.cloned.1.call-done = f32[4,64,1024]{2,1,0:T(8,128)} async-done(((f32[4,1024,1024]{2,1,0:T(8,128)}), f32[4,64,1024]{2,1,0:T(8,128)}) %reduce-scatter.29.cloned.1.call-update) | async-done | bytes 1048592 | tf_op jit(solution)/shard_map/reduce_scatter | solution.py:398
  3089.2 105.2 %all-reduce.7.cloned.1.call-done = f32[16,1024]{1,0:T(8,128)} async-done(((f32[16,1024]{1,0:T(8,128)}), f32[16,1024]{1,0:T(8,128)}) %all-reduce.7.cloned.1.call-update) | async-done | bytes 65552 | tf_op jit(solution)/shard_map/psum | solution.py:326
  3196.5 76.5 %all-gather.41.cloned.1.call-done = bf16[4,1024,1024]{2,1,0:T(8,128)(2,1)} async-done(((bf16[4,64,1024]{2,1,0:T(8,128)(2,1)}), bf16[4,1024,1024]{2,1,0:T(8,128)(2,1)}) %all-gather.41.cloned.1.call-update) | async-done | bytes 8388624 | tf_op jit(solution)/shard_map/all_gather | solution.py:399
  (522 shorter events, 731.7 us)
Async XLA Ops:
  8.0 119.4 %all-gather.21.cloned.1.call-start = ((), (), s32[]{:S(2)}) async-start(), calls=%async_computation.15 | async-start | bytes 6291456 | tf_op jit(solution)/shard_map/all_gather | solution.py:147
  8.7 200.6 %all-gather.27.cloned.1.call-start = ((), (), s32[]{:S(2)}) async-start(), calls=%async_computation.18 | async-start | bytes 9437184 | tf_op jit(solution)/shard_map/all_gather | solution.py:202
  9.5 255.7 %all-gather.19.cloned.1.call-start = ((), (), s32[]{:S(2)}) async-start(), calls=%async_computation.14 | async-start | bytes 4456448 | tf_op jit(solution)/shard_map/all_gather | solution.py:186
  77.0 239.6 %all-gather.17.cloned.1.call-start = ((), (), s32[]{:S(2)}) async-start(), calls=%async_computation.13 | async-start | bytes 4456448 | tf_op jit(solution)/shard_map/all_gather | solution.py:187
  81.2 292.0 %all-gather.23.cloned.1.call-start = ((), (), s32[]{:S(2)}) async-start(), calls=%async_computation.16 | async-start | bytes 6291456 | tf_op jit(solution)/shard_map/all_gather | solution.py:149
  81.8 444.5 %all-gather.25.cloned.1.call-start = ((), (), s32[]{:S(2)}) async-start(), calls=%async_computation.17 | async-start | bytes 18874368 | tf_op jit(solution)/shard_map/all_gather | solution.py:201
  82.6 567.3 %all-gather.31.cloned.1.call-start = ((), (), s32[]{:S(2)}) async-start(), calls=%async_computation.20 | async-start | bytes 8912896 | tf_op jit(solution)/shard_map/all_gather | solution.py:291
  546.5 153.7 %all-gather.29.cloned.1.call-start = ((), (), s32[]{:S(2)}) async-start(), calls=%async_computation.19 | async-start | bytes 8912896 | tf_op jit(solution)/shard_map/all_gather | solution.py:290
  547.3 337.1 %reduce-scatter.11.cloned.1.call-start = ((), (), s32[]{:S(2)}) async-start(), calls=%async_computation.22 | async-start | bytes 8650752 | tf_op jit(solution)/shard_map/reduce_scatter | solution.py:316
  612.6 458.7 %reduce-scatter.15.cloned.1.call-start = ((), (), s32[]{:S(2)}) async-start(), calls=%async_computation.24 | async-start | bytes 8650752 | tf_op jit(solution)/shard_map/reduce_scatter | solution.py:318
  618.3 615.8 %reduce-scatter.19.cloned.1.call-start = ((), (), s32[]{:S(2)}) async-start(), calls=%async_computation.26 | async-start | bytes 12976128 | tf_op jit(solution)/shard_map/reduce_scatter | solution.py:320
  625.9 793.4 %reduce-scatter.13.cloned.1.call-start = ((), (), s32[]{:S(2)}) async-start(), calls=%async_computation.23 | async-start | bytes 8650752 | tf_op jit(solution)/shard_map/reduce_scatter | solution.py:317
  800.8 872.8 %reduce-scatter.17.cloned.1.call-start = ((), (), s32[]{:S(2)}) async-start(), calls=%async_computation.25 | async-start | bytes 25952256 | tf_op jit(solution)/shard_map/reduce_scatter | solution.py:319
  1681.5 250.0 %reduce-scatter.21.cloned.1.call-start = ((), (), s32[]{:S(2)}) async-start(), calls=%async_computation.27 | async-start | bytes 17825792 | tf_op jit(solution)/shard_map/reduce_scatter | solution.py:398
  1753.3 254.7 %all-gather.33.cloned.1.call-start = ((), (), s32[]{:S(2)}) async-start(), calls=%async_computation.28 | async-start | bytes 8912896 | tf_op jit(solution)/shard_map/all_gather | solution.py:399
  1933.6 283.1 %reduce-scatter.23.cloned.1.call-start = ((), (), s32[]{:S(2)}) async-start(), calls=%async_computation.29 | async-start | bytes 17825792 | tf_op jit(solution)/shard_map/reduce_scatter | solution.py:398
  2039.7 253.5 %all-gather.35.cloned.1.call-start = ((), (), s32[]{:S(2)}) async-start(), calls=%async_computation.30 | async-start | bytes 8912896 | tf_op jit(solution)/shard_map/all_gather | solution.py:399
  2218.7 283.7 %reduce-scatter.25.cloned.1.call-start = ((), (), s32[]{:S(2)}) async-start(), calls=%async_computation.31 | async-start | bytes 17825792 | tf_op jit(solution)/shard_map/reduce_scatter | solution.py:398
  2325.5 253.5 %all-gather.37.cloned.1.call-start = ((), (), s32[]{:S(2)}) async-start(), calls=%async_computation.32 | async-start | bytes 8912896 | tf_op jit(solution)/shard_map/all_gather | solution.py:399
  2504.5 283.9 %reduce-scatter.27.cloned.1.call-start = ((), (), s32[]{:S(2)}) async-start(), calls=%async_computation.33 | async-start | bytes 17825792 | tf_op jit(solution)/shard_map/reduce_scatter | solution.py:398
  2611.5 253.7 %all-gather.39.cloned.1.call-start = ((), (), s32[]{:S(2)}) async-start(), calls=%async_computation.34 | async-start | bytes 8912896 | tf_op jit(solution)/shard_map/all_gather | solution.py:399
  2790.5 281.3 %reduce-scatter.29.cloned.1.call-start = ((), (), s32[]{:S(2)}) async-start(), calls=%async_computation.35 | async-start | bytes 17825792 | tf_op jit(solution)/shard_map/reduce_scatter | solution.py:398
  2894.9 299.6 %all-reduce.7.cloned.1.call-start = ((), (), s32[]{:S(2)}) async-start(), calls=%async_computation.21 | async-start | bytes 131072 | tf_op jit(solution)/shard_map/psum | solution.py:326
  2896.4 376.5 %all-gather.41.cloned.1.call-start = ((), (), s32[]{:S(2)}) async-start(), calls=%async_computation.36 | async-start | bytes 8912896 | tf_op jit(solution)/shard_map/all_gather | solution.py:399
  (101 other events, 4687.1 us)
Sparse Core Ops, SparseCore 0:
  9.6 59.4 all-gather.14
  70.6 56.7 all-gather.20
  128.9 80.3 all-gather.26
  211.9 53.2 all-gather.18
  317.9 55.2 all-gather.22
  374.7 151.5 all-gather.24
  546.7 78.0 all-gather.30
  627.0 73.2 all-gather.28
  703.0 181.3 reduce-scatter.10
  887.3 183.9 reduce-scatter.14
  1077.7 156.3 reduce-scatter.18
  1237.1 182.2 reduce-scatter.12
  1427.3 246.3 reduce-scatter.16
  1753.5 177.9 reduce-scatter.20
  1934.1 73.9 all-gather.32
  2039.8 176.7 reduce-scatter.22
  2219.2 73.9 all-gather.34
  2325.6 176.7 reduce-scatter.24
  2505.0 73.9 all-gather.36
  2611.6 176.7 reduce-scatter.26
  2791.2 73.9 all-gather.38
  2895.0 176.8 reduce-scatter.28
  3077.9 116.5 all-reduce.6
  3197.2 75.7 all-gather.40
  (1 shorter events, 48.7 us)
where the time goes:
time: 3340 us; the launch traced here: 3330 us
  waiting for transfers between devices  2670 us (80%)
  matrix products  353 us (11%)
  local copies, waits for them, and re-layouts  119 us (4%)
  other arithmetic  93 us (3%)
  blocking collectives  67.6 us (2%)
    reduce_scatter x5, waiting for transfers between devices, on_device(): lax.psum_scatter(partial_gram, 'ctx', scatter_dimension=1, tiled=True)  884 us
    all_gather x5, waiting for transfers between devices, on_device(): lax.all_gather(gram_part.astype(jnp.bfloat16), 'ctx', axis=1, tiled=True)  373 us
    reduce_scatter x1, waiting for transfers between devices, on_device(): lax.psum_scatter(grad_gateup, ('ctx', 'wt'), scatter_dimension=1, tiled=T...  253 us
    reduce_scatter x1, waiting for transfers between devices, on_device(): lax.psum_scatter(grad_outproj, ('ctx', 'wt'), scatter_dimension=0, tiled=...  185 us
    reduce_scatter x1, waiting for transfers between devices, on_device(): lax.psum_scatter(grad_keyval, ('ctx', 'wt'), scatter_dimension=1, tiled=T...  182 us
    reduce_scatter x1, waiting for transfers between devices, on_device(): lax.psum_scatter(grad_down, ('ctx', 'wt'), scatter_dimension=0, tiled=True)  161 us
    all_gather x1, waiting for transfers between devices, on_device(): lax.all_gather(w_gateup, 'wt', axis=1, tiled=True)  150 us
    psum x1, waiting for transfers between devices, on_device(): lax.psum((norm_terms, head_terms, grad_gate_head), ('ctx', 'wt'))  105 us
  transfers between devices with their start and end apart: 27, of which 24 were waited for; matrix products, arithmetic and copies ran while one was open for 11% of the time, Pallas kernels for 0%

commit v1 on v0

v1 whole, which is shorter than its diff:
```python
import functools
import math

import jax
import jax.numpy as jnp
from jax import lax
from jax.experimental import pallas as pl
from jax.experimental.pallas import tpu as pltpu
from jax.sharding import Mesh, PartitionSpec as P

NS_STEPS = 5
NORM_EPS = 1e-06
ROPE_BASE = 1000000.0
NS_A = 3.4445
NS_B = -4.775
NS_C = 2.0315
MATRIX_RATE = 0.03
VECTOR_RATE = 0.003
CTX = ("h", "m", "i", "b", "c")
ALL = CTX + ("x",)
F32 = jnp.float32
BF16 = jnp.bfloat16


def nt(p, q):
    return lax.dot_general(p, q, (((1,), (1,)), ((), ())), preferred_element_type=F32)


def nn(p, q):
    return lax.dot_general(p, q, (((1,), (0,)), ((), ())), preferred_element_type=F32)


def tn(p, q):
    return lax.dot_general(p, q, (((0,), (0,)), ((), ())), preferred_element_type=F32)


def flip(v, *axes):
    last = 2 ** len(axes) - 1
    return lax.ppermute(v, tuple(sorted(axes, key=ALL.index)), [(j, j ^ last) for j in range(last + 1)])


NEAR = (("x",), ("b",), ("b", "x"))


def gather_near(v):
    return [v] + [flip(v, *axes) for axes in NEAR]


def pieces_far(near):
    return near + [flip(member, "c") for member in near]


def join_kernel(*refs):
    ins, out, sems = refs[:-2], refs[-2], refs[-1]
    rows = ins[0].shape[0]
    run_copies([(ref, out.at[pl.ds(k * rows, rows)]) for k, ref in enumerate(ins)], sems)


def join(pieces):
    rows, width = pieces[0].shape
    count = len(pieces)
    return pl.pallas_call(
        join_kernel,
        out_shape=jax.ShapeDtypeStruct((count * rows, width), pieces[0].dtype),
        in_specs=[HBM_SPEC] * count,
        out_specs=VMEM_SPEC,
        scratch_shapes=[pltpu.SemaphoreType.DMA((count,))],
        compiler_params=SMALL,
        cost_estimate=pl.CostEstimate(
            flops=0, bytes_accessed=4 * count * rows * width, transcendentals=0
        ),
        name="join",
    )(*pieces)


def gather_far(near):
    return join(pieces_far(near))


def gather_group(v):
    return gather_far(gather_near(v))


def sum_core(part):
    half = part.shape[0] // 2
    return part[:half] + flip(part[half:].astype(BF16), "c").astype(F32)


def sum_near(part):
    rows = part.shape[0] // 4
    low = part.astype(BF16)
    total = part[:rows]
    for slot, axes in enumerate(NEAR, 1):
        total = total + flip(low[slot * rows : (slot + 1) * rows], *axes).astype(F32)
    return total


def sum_group(part):
    return sum_near(sum_core(part))


def sum_flips(v, flips):
    return sum((flip(v, *axes) for axes in flips), v)


def swap_halves(v, my_half, my_x):
    other = lax.ppermute(v, ("h", "x"), [(1, 2), (2, 1)])
    return jnp.where(my_half == my_x, v, other)


DOWN, NONE, GATE, UP = range(4)
QUERY, OUT, KEY, VALUE = range(4)

def trade(v, axes):
    return lax.all_to_all(v, axes, split_axis=0, concat_axis=0, tiled=True)


def turned(v):
    return jnp.stack([v[0], v[2], v[1], v[3]])


def fold_pairs(q):
    return [(i * 2 + b, b * q + i) for i in range(q) for b in range(2)]


def to_home(items, q, token):
    if q > 1:
        items = lax.ppermute(items, ("i", "b"), [(d, s) for s, d in fold_pairs(q)])
    return trade(turned(tie(trade(items, ("h", "m")), token)), ("c", "x"))


def to_owner(blocks, q, token):
    items = trade(tie(turned(trade(blocks, ("c", "x"))), token), ("h", "m"))
    if q > 1:
        items = lax.ppermute(items, ("i", "b"), fold_pairs(q))
    return items


VMEM_SPEC = pl.BlockSpec(memory_space=pltpu.VMEM)
SMEM_SPEC = pl.BlockSpec(memory_space=pltpu.SMEM)
SMALL = pltpu.CompilerParams(vmem_limit_bytes=32 * 2**20)
LARGE = pltpu.CompilerParams(vmem_limit_bytes=60 * 2**20)


HBM_SPEC = pl.BlockSpec(memory_space=pl.ANY)
FAR_SPEC = pl.BlockSpec(memory_space=pltpu.HBM)


def run_copies(pairs, sems):
    copies = [pltpu.make_async_copy(p, q, sems.at[k]) for k, (p, q) in enumerate(pairs)]
    for copy in copies:
        copy.start()
    for copy in copies:
        copy.wait()


def slices_kernel(sub_ref, wq, wkv, wo, wgu, wd, gate, w_in, o_out, gu_out, d_out, sems):
    sub = sub_ref[0, 0]
    q_rows, kv_rows = o_out.shape[0], wkv.shape[1] // 4

    def part(ref, rows):
        return ref.at[pl.ds(pl.multiple_of(sub * rows, rows), rows)]

    pairs = [
        (part(wq, q_rows), w_in.at[pl.ds(0, q_rows)]),
        (part(wkv.at[0], kv_rows), w_in.at[pl.ds(q_rows, kv_rows)]),
        (part(wkv.at[1], kv_rows), w_in.at[pl.ds(q_rows + kv_rows, kv_rows)]),
        (gate, w_in.at[pl.ds(q_rows + 2 * kv_rows, gate.shape[0])]),
        (part(wo, q_rows), o_out),
    ]
    pairs += [(part(wgu.at[g], d_out.shape[0]), gu_out.at[g]) for g in range(2)]
    pairs.append((part(wd, d_out.shape[0]), d_out))
    run_copies(pairs, sems)


def weight_slices(sub, w_query, w_keyval, w_outproj, w_gateup, w_down, gate):
    width = w_query.shape[1]
    q_rows, kv_rows = w_query.shape[0] // 4, w_keyval.shape[1] // 4
    ff_rows = w_down.shape[0] // 4
    w_in, wo, wgu, wd = pl.pallas_call(
        slices_kernel,
        out_shape=[
            jax.ShapeDtypeStruct((q_rows + 2 * kv_rows + gate.shape[0], width), BF16),
            jax.ShapeDtypeStruct((q_rows, width), BF16),
            jax.ShapeDtypeStruct((2, ff_rows, width), BF16),
            jax.ShapeDtypeStruct((ff_rows, width), BF16),
        ],
        in_specs=[SMEM_SPEC] + [FAR_SPEC] * 5 + [HBM_SPEC],
        out_specs=[VMEM_SPEC] * 4,
        scratch_shapes=[pltpu.SemaphoreType.DMA((8,))],
        compiler_params=LARGE,
        cost_estimate=pl.CostEstimate(flops=0, bytes_accessed=2**23, transcendentals=0),
        name="slices",
    )(
        sub.reshape(1, 1),
        w_query,
        w_keyval,
        w_outproj,
        w_gateup,
        w_down,
        gate,
    )
    return w_in, wo, wgu.reshape(2 * ff_rows, width), wd


def owned_kernel(spot_ref, *refs):
    ins, outs, sems = refs[:5], refs[-3:-1], refs[-1]
    pairs = []
    for k, out in enumerate(outs):
        spot, at = spot_ref[0, k], 0
        for ref in ins:
            rows = ref.shape[-2] // row_blocks(out, ins)
            span = pl.ds(pl.multiple_of(spot * rows, rows), rows)
            for part in [ref.at[j] for j in range(2)] if len(ref.shape) == 3 else [ref]:
                pairs.append((part.at[span], out.at[pl.ds(at, rows)]))
                at += rows
    run_copies(pairs, sems)


def row_blocks(out, ins):
    total = sum(ref.shape[-2] * (2 if len(ref.shape) == 3 else 1) for ref in ins)
    return total // out.shape[0]


def owned_rows(spots, weights, n, *tokens):
    rows = sum(w.shape[-2] * (2 if w.ndim == 3 else 1) for w in weights) // (4 * n)
    out = jax.ShapeDtypeStruct((rows, weights[0].shape[-1]), BF16)
    return pl.pallas_call(
        owned_kernel,
        out_shape=[out, out],
        in_specs=[SMEM_SPEC] + [FAR_SPEC] * 5 + [HBM_SPEC] * len(tokens),
        out_specs=[VMEM_SPEC] * 2,
        scratch_shapes=[pltpu.SemaphoreType.DMA((14,))],
        compiler_params=LARGE,
        cost_estimate=pl.CostEstimate(flops=0, bytes_accessed=2**22, transcendentals=0),
        name="owned",
    )(spots, *weights, *tokens)


def tie(value, *tokens):
    return pl.pallas_call(
        lambda *refs: None,
        out_shape=jax.ShapeDtypeStruct(value.shape, value.dtype),
        in_specs=[HBM_SPEC] * (1 + len(tokens)),
        out_specs=HBM_SPEC,
        input_output_aliases={0: 0},
        cost_estimate=pl.CostEstimate(flops=0, bytes_accessed=0, transcendentals=0),
        name="tie",
    )(value, *tokens)


def pack_kernel(places, ins, *refs):
    out = refs[-1]
    height, width = out.shape[1:]
    filled = set()
    for ref, item in zip(refs[:ins], places):
        rows = ref.shape[-2]
        for j, member in enumerate(item):
            source = ref[j] if len(ref.shape) == 3 else ref[...]
            out[member, :rows] = source.astype(BF16)
            if rows < height:
                out[member, rows:] = jnp.zeros((height - rows, width), BF16)
            filled.add(member)
    for member in range(4):
        if member not in filled:
            out[member] = jnp.zeros((height, width), BF16)


def pack(arrays, places, height, *tokens):
    width = arrays[0].shape[-1]
    return pl.pallas_call(
        functools.partial(pack_kernel, places, len(arrays)),
        out_shape=jax.ShapeDtypeStruct((4, height, width), BF16),
        in_specs=[VMEM_SPEC] * len(arrays) + [HBM_SPEC] * len(tokens),
        out_specs=VMEM_SPEC,
        compiler_params=SMALL,
        cost_estimate=pl.CostEstimate(flops=0, bytes_accessed=24 * height * width, transcendentals=0),
        name="pack",
    )(*arrays, *tokens)


def held_kernel(v_ref, *refs):
    refs[-1][...] = v_ref[...]


def held(v, *tokens):
    return pl.pallas_call(
        held_kernel,
        out_shape=jax.ShapeDtypeStruct(v.shape, v.dtype),
        in_specs=[VMEM_SPEC] + [HBM_SPEC] * len(tokens),
        out_specs=VMEM_SPEC,
        compiler_params=SMALL,
        cost_estimate=pl.CostEstimate(flops=0, bytes_accessed=4 * v.size, transcendentals=0),
        name="held",
    )(v, *tokens)


def settle_kernel(places, rates, items, *refs):
    if rates is None:
        count = len(places)
        olds, outs = refs[:count], refs[count:]
    else:
        old_ref, outs = refs[0], refs[1:]
    for a, item in enumerate(places):
        rows = outs[a].shape[-2]
        for j, place in enumerate(item):
            at = (j,) if len(outs[a].shape) == 3 else (slice(None),)
            member, first = place if rates is not None else (place, 0)
            value = items[member, :rows].astype(F32)
            if rates is None:
                outs[a][at] = value
                outs[count + a][at] = 0.5 * olds[a][at] + 0.5 * value
            else:
                old = old_ref[first : first + rows, :].astype(F32)
                outs[a][at] = old - rates[member] * value


def settle(items, olds, shapes, places, rates):
    shapes = [jax.ShapeDtypeStruct(v.shape, F32) for v in shapes]
    shapes = shapes * (2 if rates is None else 1)
    return pl.pallas_call(
        functools.partial(settle_kernel, places, rates),
        out_shape=shapes,
        in_specs=[VMEM_SPEC] * (1 + len(olds)),
        out_specs=[VMEM_SPEC] * len(shapes),
        compiler_params=SMALL,
        cost_estimate=pl.CostEstimate(flops=0, bytes_accessed=12 * items.size, transcendentals=0),
        name="settle",
    )(items, *olds)


TILE = 512


def tile_at(j):
    return pl.ds(pl.multiple_of(j * TILE, TILE), TILE)


def attend_kernel(scale, q_ref, k_ref, v_ref, qp_ref, kp_ref, o_ref):
    @pl.loop(0, q_ref.shape[0] // TILE)
    def _(i):
        query, place = q_ref[tile_at(i), :], qp_ref[tile_at(i), :]

        def step(j, acc):
            scores = nt(query, k_ref[tile_at(j), :])
            weights = jnp.where(kp_ref[:, tile_at(j)] <= place, jnp.exp2(scores * scale), 0.0)
            return acc + nn(weights.astype(BF16), v_ref[tile_at(j), :])

        o_ref[tile_at(i), :] = lax.fori_loop(
            0, k_ref.shape[0] // TILE, step, jnp.zeros((TILE, v_ref.shape[1]), F32)
        )


def attend(query, key, wide, q_place, k_place, scale):
    rows, dim = query.shape
    keys = key.shape[0]
    out = pl.pallas_call(
        functools.partial(attend_kernel, scale * math.log2(math.e)),
        out_shape=jax.ShapeDtypeStruct((rows, 2 * dim), F32),
        in_specs=[VMEM_SPEC] * 5,
        out_specs=VMEM_SPEC,
        compiler_params=pltpu.CompilerParams(vmem_limit_bytes=40 * 2**20),
        cost_estimate=pl.CostEstimate(
            flops=22 * rows * keys * dim, bytes_accessed=rows * dim * 12, transcendentals=0
        ),
        name="attend",
    )(query, key, wide, q_place[:, None], k_place[None, :])
    return out[:, :dim], out[:, dim : dim + 1]


def attend_back_kernel(
    scale, q_ref, w_ref, cr_ref, qp_ref, k_ref, v_ref, kp_ref, dq_ref, dk_ref, dv_ref
):
    dk_ref[...] = jnp.zeros_like(dk_ref)
    dv_ref[...] = jnp.zeros_like(dv_ref)
    grow = scale * math.log2(math.e)

    @pl.loop(0, q_ref.shape[0] // TILE)
    def _(i):
        query, back = q_ref[tile_at(i), :], w_ref[tile_at(i), :]
        place, corr = qp_ref[:, tile_at(i)], cr_ref[:, tile_at(i)]

        def step(j, acc):
            span = tile_at(j)
            key = k_ref[span, :]
            weights = jnp.where(kp_ref[span, :] <= place, jnp.exp2(nt(key, query) * grow), 0.0)
            push = nt(v_ref[span, :], back)
            dscore = (weights * (push - corr) * scale).astype(BF16)
            dv_ref[span, :] += nn(weights.astype(BF16), back)
            dk_ref[span, :] += nn(dscore, query)
            return acc + tn(dscore, key)

        dq_ref[tile_at(i), :] = lax.fori_loop(
            0, k_ref.shape[0] // TILE, step, jnp.zeros(query.shape, F32)
        )


def attend_back(query, back, corr, key, value, q_place, k_place, scale):
    rows, dim = query.shape
    keys = key.shape[0]
    return pl.pallas_call(
        functools.partial(attend_back_kernel, scale),
        out_shape=(
            jax.ShapeDtypeStruct((rows, dim), F32),
            jax.ShapeDtypeStruct((keys, dim), F32),
            jax.ShapeDtypeStruct((keys, dim), F32),
        ),
        in_specs=[VMEM_SPEC] * 7,
        out_specs=[VMEM_SPEC] * 3,
        compiler_params=pltpu.CompilerParams(vmem_limit_bytes=40 * 2**20),
        cost_estimate=pl.CostEstimate(
            flops=40 * rows * keys * dim, bytes_accessed=rows * dim * 16, transcendentals=0
        ),
        name="attend_back",
    )(query, back, corr[None, :], q_place[None, :], key, value, k_place[:, None])


def rms_scale(v):
    return lax.rsqrt(jnp.mean(v * v, axis=-1, keepdims=True) + NORM_EPS)


def rotate(v, cosine, sine):
    half = v.shape[-1] // 2
    lead, trail = v[..., :half], v[..., half:]
    return jnp.concatenate([lead * cosine - trail * sine, trail * cosine + lead * sine], axis=-1)


def rotate_back(g, cosine, sine):
    half = g.shape[-1] // 2
    lead, trail = g[..., :half], g[..., half:]
    return jnp.concatenate([lead * cosine + trail * sine, trail * cosine - lead * sine], axis=-1)


def norm_back(grad, scaled, rscale, gains):
    pushed = grad * gains
    return rscale * (pushed - scaled * jnp.mean(pushed * scaled, axis=-1, keepdims=True))


def mirror(ref, tile):
    for j in range(ref.shape[0] // tile):
        for i in range(j):
            block = ref[i * tile : (i + 1) * tile, j * tile : (j + 1) * tile].astype(F32)
            ref[j * tile : (j + 1) * tile, i * tile : (i + 1) * tile] = block.T.astype(BF16)


def schulz_kernel(count, start_ref, *refs):
    pieces = refs[:count]
    o_ref, x_ref, x_own, e_gram, e_poly, e_half, gram, poly, half, sems = refs[-10:]
    piece = pieces[0].shape[0]
    copies = [
        pltpu.make_async_copy(ref, x_ref.at[pl.ds(k * piece, piece)], sems.at[k])
        for k, ref in enumerate(pieces)
    ]
    for copy in copies:
        copy.start()
    for copy in copies:
        copy.wait()
    chunk = min(1024, x_ref.shape[0])
    width = x_ref.shape[1]
    own = o_ref.shape[0]
    tile = 256
    blocks = [(slice(0, (j + 1) * tile), slice(j * tile, (j + 1) * tile)) for j in range(width // tile)]
    diag = (
        lax.broadcasted_iota(jnp.int32, (tile, tile), 0)
        == lax.broadcasted_iota(jnp.int32, (tile, tile), 1)
    ).astype(F32)

    def trace(ref):
        total = jnp.zeros((tile, tile), F32)
        for _, cols in blocks:
            total = total + ref[cols, cols] * diag
        return jnp.sum(jnp.sum(total, axis=1, keepdims=True), axis=0, keepdims=True)

    def settle_gram(scale, centre):
        for rows, cols in blocks:
            part = e_gram[rows, cols]
            e_gram[rows, cols] = part if scale is None else part * scale
            e_gram[cols, cols] -= centre * diag
            gram[rows, cols] = e_gram[rows, cols].astype(BF16)
        mirror(gram, tile)

    def make_poly(d):
        p = NS_A + NS_B * d + NS_C * d * d
        for rows, cols in blocks:
            part = (NS_B + 2.0 * NS_C * d) * e_gram[rows, cols] + NS_C * nn(
                gram[rows, :], gram[:, cols]
            )
            e_poly[rows, cols] = part
            poly[rows, cols] = part.astype(BF16)
        mirror(poly, tile)
        return p

    def advance(d, p):
        for rows, cols in blocks:
            part = d * e_poly[rows, cols] + p * e_gram[rows, cols] + nn(gram[rows, :], poly[:, cols])
            e_half[rows, cols] = part
            half[rows, cols] = part.astype(BF16)
        mirror(half, tile)
        q = d * p
        for rows, cols in blocks:
            e_gram[rows, cols] = (
                q * e_poly[rows, cols] + p * e_half[rows, cols] + nn(half[rows, :], poly[:, cols])
            )
        centre = trace(e_gram) * (1.0 / width)
        settle_gram(None, centre)
        return q * p + centre

    def apply(p):
        now = x_own[...]
        return p * now + nn(now.astype(BF16), poly[...])

    for rows, cols in blocks:
        e_gram[rows, cols] = lax.fori_loop(
            0,
            x_ref.shape[0] // chunk,
            lambda r, acc: acc
            + tn(
                x_ref[pl.ds(pl.multiple_of(r * chunk, chunk), chunk), rows],
                x_ref[pl.ds(pl.multiple_of(r * chunk, chunk), chunk), cols],
            ),
            jnp.zeros((rows.stop, tile), F32),
        )
    square = trace(e_gram)
    inv = 1.0 / (jnp.sqrt(square) + 1e-07)
    first = square * inv * inv * (1.0 / width)
    settle_gram(inv * inv, first)
    rows = own // 4
    for k in range(4):
        block = x_ref[pl.ds(pl.multiple_of(start_ref[0, k], rows), rows), :]
        x_own[k * rows : (k + 1) * rows, :] = block.astype(F32) * inv

    def sweep(_, d):
        p = make_poly(d)
        x_own[...] = apply(p)
        return advance(d, p)

    d = lax.fori_loop(0, NS_STEPS - 1, sweep, first)
    o_ref[...] = apply(make_poly(d)).astype(BF16)


def orthogonal(pieces, firsts, own, *tokens):
    count = len(pieces)
    rows, width = count * pieces[0].shape[0], pieces[0].shape[1]
    wide = pltpu.VMEM((width, width), F32)
    low = pltpu.VMEM((width, width), BF16)
    return pl.pallas_call(
        functools.partial(schulz_kernel, count),
        out_shape=jax.ShapeDtypeStruct((own, width), BF16),
        in_specs=[SMEM_SPEC] + [HBM_SPEC] * (count + len(tokens)),
        out_specs=VMEM_SPEC,
        scratch_shapes=[
            pltpu.VMEM((rows, width), BF16),
            pltpu.VMEM((own, width), F32),
            wide,
            wide,
            wide,
            low,
            low,
            low,
            pltpu.SemaphoreType.DMA((count,)),
        ],
        compiler_params=pltpu.CompilerParams(vmem_limit_bytes=48 * 2**20),
        cost_estimate=pl.CostEstimate(
            flops=44 * 2**30, bytes_accessed=4 * rows * width, transcendentals=0
        ),
        name="schulz",
    )(firsts, *pieces, *tokens)


def on_device(
    n,
    tokens,
    cotangent,
    pair_order,
    norm_gains,
    head_gains,
    gate_head,
    w_query,
    w_keyval,
    w_outproj,
    w_gateup,
    w_down,
    mom_norm,
    mom_head,
    mom_gate_head,
    mom_query,
    mom_keyval,
    mom_outproj,
    mom_gateup,
    mom_down,
):
    quarter = n // 4
    my_h, my_m, my_i = lax.axis_index("h"), lax.axis_index("m"), lax.axis_index("i")
    my_b, my_c, my_x = lax.axis_index("b"), lax.axis_index("c"), lax.axis_index("x")
    me = lax.axis_index(ALL)
    everywhere = ("h", "m", "i")
    sub = my_c * 2 + my_b
    my_plane = my_h * 2 + my_m
    tok_dev, width = tokens.shape[1], tokens.shape[2]
    head_dim = head_gains.shape[1]
    scale = 1.0 / math.sqrt(head_dim)
    piece = tok_dev // 2
    group_rows = 8 * tok_dev

    rows_tok = swap_halves(tokens[0], my_h, my_x)
    xf = rows_tok.astype(F32)
    r1 = rms_scale(xf)
    y1 = xf * r1
    normed_rows = (y1 * norm_gains[0]).astype(BF16)
    q_rows = w_query.shape[0] // 4
    kv_rows = w_keyval.shape[1] // 4
    heads_here = q_rows // head_dim
    wgate = lax.dynamic_slice_in_dim(gate_head, (my_x * 4 + sub) * heads_here, heads_here, 0)
    gate_pad = 128 - heads_here
    small_block = w_keyval.shape[1] // (4 * n)
    out_block = w_outproj.shape[0] // (4 * n)
    ff_block = w_gateup.shape[1] // (4 * n)
    ff_rows = n * ff_block
    w_in, wo, wgu, wd = weight_slices(
        sub,
        w_query,
        w_keyval,
        w_outproj,
        w_gateup,
        w_down,
        jnp.pad(wgate, ((0, gate_pad), (0, 0))),
    )


    order_ids = jnp.arange(pair_order.shape[0], dtype=jnp.int32)

    def group_place(r_index):
        flips = jnp.arange(8, dtype=jnp.int32)
        dev_x = my_x ^ (flips & 1)
        dev_b = my_b ^ ((flips >> 1) & 1)
        dev_c = my_c ^ (flips >> 2)
        ctx_ids = ((dev_x * (n // 2) + r_index) * 2 + dev_b) * 2 + dev_c
        owner = jnp.sum(
            jnp.where(ctx_ids[:, None] == order_ids[None, :], pair_order[None, :], 0), axis=1
        )
        blocks = jnp.stack([owner, 2 * pair_order.shape[0] - 1 - owner], axis=1)
        spots = blocks[:, :, None] * piece + jnp.arange(piece, dtype=jnp.int32)
        return spots.reshape(group_rows)

    my_r = my_m * quarter + my_i
    place = group_place(my_r)
    if n == 4:
        key_place = jnp.concatenate([place, group_place(my_r ^ 1)])
    else:
        key_place = jnp.concatenate([group_place(r) for r in range(n // 2)])

    def gather_keys(v):
        if n == 4:
            return jnp.concatenate([v, flip(v, "m")], axis=0)
        return lax.all_gather(v, ("m", "i"), axis=0, tiled=True)

    def sum_keys(v):
        if n == 4:
            return v[:group_rows] + flip(v[group_rows:].astype(BF16), "m").astype(F32)
        return lax.psum_scatter(v, ("m", "i"), scatter_dimension=0, tiled=True)

    inverse = ROPE_BASE ** (-(2.0 * jnp.arange(head_dim // 2, dtype=F32)) / head_dim)
    angles = place.astype(F32)[:, None] * inverse[None, :]
    cosine, sine = jnp.cos(angles), jnp.sin(angles)
    normed_rows = tie(normed_rows, w_in, cosine, key_place)
    normed = gather_group(normed_rows)
    projected = nt(normed, w_in)
    rows_cot = swap_halves(held(cotangent[0], normed_rows), my_h, my_x)
    cot_near = gather_near(tie(rows_cot, projected))
    query_raw = jnp.stack(
        [projected[:, j * head_dim : (j + 1) * head_dim] for j in range(heads_here)]
    )
    key_raw = projected[:, q_rows : q_rows + kv_rows]
    value_rows = projected[:, q_rows + kv_rows : q_rows + 2 * kv_rows].astype(BF16)
    logits = projected[:, q_rows + 2 * kv_rows : q_rows + 2 * kv_rows + heads_here]
    rq, rk = rms_scale(query_raw), rms_scale(key_raw)
    yq, yk = query_raw * rq, key_raw * rk
    query_rows = rotate(yq * head_gains[0], cosine, sine).astype(BF16)
    key_rows = rotate(yk * head_gains[1], cosine, sine).astype(BF16)
    key_all, value_all = gather_keys(key_rows), gather_keys(value_rows)
    flat_query = query_rows.reshape(heads_here * group_rows, head_dim)
    flat_place = jnp.tile(place, heads_here)
    wide = jnp.concatenate([value_all, jnp.ones_like(value_all)], axis=1)
    summed, total = attend(flat_query, key_all, wide, flat_place, key_place, scale)
    attended = (summed / total).reshape(heads_here, group_rows, head_dim)
    total = total.reshape(heads_here, group_rows, 1)
    gate_sig = jax.nn.sigmoid(logits).T[:, :, None]
    gated = attended * gate_sig
    gated = jnp.concatenate([gated[j] for j in range(heads_here)], axis=1).astype(BF16)
    middle = xf + sum_group(nn(gated, wo))
    grad_all = gather_far(cot_near)
    r2 = rms_scale(middle)
    y2 = middle * r2
    hidden_in = gather_group((y2 * norm_gains[1]).astype(BF16))
    gate_up = nt(hidden_in, wgu)
    gate_part, up_part = gate_up[:, :ff_rows], gate_up[:, ff_rows:]
    sg = jax.nn.sigmoid(gate_part)
    silu = gate_part * sg
    hidden = (silu * up_part).astype(BF16)

    dhidden = nt(grad_all, wd)
    dgu = jnp.concatenate(
        [
            (dhidden * up_part * sg * (1.0 + gate_part * (1.0 - sg))).astype(BF16),
            (dhidden * silu).astype(BF16),
        ],
        axis=1,
    )
    grad_gu = tn(dgu, hidden_in).astype(BF16)
    grad_d = tn(hidden, grad_all).astype(BF16)
    ff_grad = lax.psum_scatter(
        jnp.concatenate([grad_d, jnp.zeros_like(grad_d), grad_gu], axis=0),
        ("h", "m", "i"),
        scatter_dimension=0,
        tiled=True,
    )
    dhn = sum_group(nn(dgu, wgu))
    gout = rows_cot.astype(F32)
    norm_terms_mid = jnp.sum(dhn * y2, axis=0)
    dmiddle = gout + norm_back(dhn, y2, r2, norm_gains[1])
    dbranch = gather_group(dmiddle.astype(BF16))

    first_moms = (mom_gateup, mom_down)
    first_places = ((GATE, UP), (DOWN,))
    second_moms = (mom_query, mom_keyval, mom_outproj)
    second_places = ((QUERY,), (KEY, VALUE), (OUT,))
    first_pack = pack(first_moms, first_places, ff_block, middle)
    second_pack = pack(second_moms, second_places, out_block, gate_up)
    first_old = to_home(first_pack, quarter, dhn)
    second_old = to_home(second_pack, quarter, dbranch)

    spot = me % (4 * n)
    mine_now, other_now = owned_rows(
        jnp.stack([spot, spot ^ 1]).reshape(1, 2),
        (w_query, w_keyval, w_outproj, w_gateup, w_down),
        n,
        dbranch,
    )
    old_rows = jnp.where(my_x == my_h, mine_now, flip(other_now, "x"))

    dgated = nt(dbranch, wo)
    def over_i(v):
        return lax.psum_scatter(v, "i", scatter_dimension=0, tiled=True) if quarter > 1 else v

    def to_out_plane(v):
        v = v.astype(F32) + lax.ppermute(v, ("h", "m"), [(0, 1), (3, 2)]).astype(F32)
        return v + lax.ppermute(v.astype(BF16), ("h", "m"), [(2, 1)]).astype(F32)

    def to_block(v):
        v = v.reshape(-1, width)
        return jnp.concatenate(
            [v]
            + [
                lax.ppermute(v, "i", [((j + d) % quarter, j) for j in range(quarter)])
                for d in range(1, quarter)
            ],
            axis=0,
        )

    def blend(old, grad):
        return (0.5 * old.astype(F32) + 0.5 * grad.astype(F32)).astype(BF16)

    def padded(v, rows, height):
        blocks = v.reshape(4, rows, width)
        return jnp.pad(blocks, ((0, 0), (0, height - rows), (0, 0)))

    position = my_b * 1 + my_i * 2
    source_b, source_i = position // quarter, position % quarter

    def firsts(rows, mine_first):
        return jnp.stack(
            [
                (
                    (((my_c ^ m) * 2 + (source_b ^ my_b)) * 2 + (my_x ^ h))
                    if mine_first
                    else (source_b * 2 + m) * 2 + h
                )
                * (4 * quarter * rows)
                + ((source_i - my_i) % quarter) * (4 * rows)
                + (my_c * 2 + my_x) * rows
                for h in range(2)
                for m in range(2)
            ]
        ).reshape(1, 4)

    grad_o = to_out_plane(over_i(tn(gated, dbranch).astype(BF16)))
    first_grad = ff_grad.reshape(4, ff_block, width)
    first_mine = blend(first_old, first_grad)
    out_sum = sum_core(nn(hidden, wd))

    dgated = jnp.stack([dgated[:, j * head_dim : (j + 1) * head_dim] for j in range(heads_here)])
    dattended = dgated * gate_sig
    dlogit = (
        gate_sig * (1.0 - gate_sig) * jnp.sum(dgated * attended, axis=-1, keepdims=True)
    ).astype(BF16)
    corr = jnp.sum(dattended * attended, axis=-1, keepdims=True) / total
    back_w = (dattended / total).astype(BF16)
    dquery, dkey_part, dvalue_part = attend_back(
        flat_query,
        back_w.reshape(heads_here * group_rows, head_dim),
        corr.reshape(heads_here * group_rows),
        key_all,
        value_all,
        flat_place,
        key_place,
        scale,
    )
    out_rows = middle + sum_near(out_sum)
    dkey_part = tie(dkey_part, out_rows)
    first_block = to_block(first_mine)
    first_start = lax.all_gather(first_block, ("b", "c", "x"), axis=0, tiled=True)
    dkey, dvalue = sum_keys(dkey_part), sum_keys(dvalue_part)
    dqn = rotate_back(dquery.reshape(heads_here, group_rows, head_dim), cosine, sine)
    dkn = rotate_back(dkey, cosine, sine)
    head_terms = jnp.stack([jnp.sum(dqn * yq, axis=(0, 1)), jnp.sum(dkn * yk, axis=0)])
    dq = norm_back(dqn, yq, rq, head_gains[0]).astype(BF16)
    dk = norm_back(dkn, yk, rk, head_gains[1]).astype(BF16)
    dall = jnp.concatenate(
        [dq[j] for j in range(heads_here)]
        + [dk, dvalue.astype(BF16)]
        + [dlogit[j] for j in range(heads_here)]
        + [jnp.zeros((group_rows, gate_pad), BF16)],
        axis=1,
    )
    dall = tie(dall, second_old, grad_o)
    grad_in = tn(dall, normed)
    query_part = grad_in[:q_rows].reshape(n, 2, small_block, width)
    second_part = jnp.concatenate(
        [
            jnp.transpose(query_part, (1, 0, 2, 3)).reshape(q_rows, width),
            grad_in[q_rows : q_rows + 2 * kv_rows],
        ],
        axis=0,
    ).astype(BF16)
    dnormed = sum_near(sum_core(nn(dall, w_in)))
    norm_terms_in = jnp.sum(dnormed * y1, axis=0)
    grad_rows = dmiddle + norm_back(dnormed, y1, r1, norm_gains[0])
    if quarter > 1:
        second_part = second_part.reshape(4, quarter, -1, width)
        second_part = lax.psum_scatter(second_part, "i", scatter_dimension=1, tiled=True)
    second_part = second_part.reshape(4, 4 * small_block, width)
    first_mid = turned(trade(first_grad, ("c", "x")))
    chunks = [
        lax.dynamic_index_in_dim(second_part, my_plane ^ k, 0, keepdims=False) for k in range(4)
    ]
    mine = chunks[0].astype(F32)
    for k, axes in ((1, ("m",)), (2, ("h",)), (3, ("h", "m"))):
        mine = mine + flip(chunks[k], *axes).astype(F32)
    mine = tie(mine.astype(BF16), first_mid, old_rows)
    pair = flip(mine, "m")
    mine, pair = (v.reshape(4, small_block, width) for v in (mine, pair))
    second_grad = jnp.concatenate(
        [mine, jnp.where(my_plane == QUERY, pair, jnp.zeros_like(pair))], axis=1
    )
    second_grad = jnp.where(
        my_plane == OUT, grad_o.astype(BF16).reshape(4, out_block, width), second_grad
    )
    second_block = to_block(blend(second_old, second_grad))
    small_z = sum_flips(
        jnp.concatenate(
            [
                lax.dynamic_update_slice_in_dim(
                    jnp.zeros((gate_head.shape[0], width), F32),
                    grad_in[q_rows + 2 * kv_rows : q_rows + 2 * kv_rows + heads_here],
                    (my_x * 4 + sub) * heads_here,
                    0,
                ),
                norm_terms_in[None],
                norm_terms_mid[None],
                jnp.pad(head_terms.reshape(1, 2 * head_dim), ((0, 0), (0, width - 2 * head_dim))),
            ],
            axis=0,
        ),
        (("m",), ("h",), ("h", "m")),
    )
    if quarter > 1:
        small_z = lax.psum(small_z, "i")
    second_near = gather_near(second_block)
    output = swap_halves(tie(out_rows.astype(BF16), dall), my_h, my_x)
    first_g = trade(tie(first_mid, second_block), ("h", "m"))
    if quarter > 1:
        first_g = lax.ppermute(first_g, ("i", "b"), fold_pairs(quarter))
    first_ortho = orthogonal(
        [first_start], firsts(ff_block, False), 4 * ff_block, second_block
    )
    second_ortho = orthogonal(
        pieces_far([tie(v, first_ortho) for v in second_near]), firsts(out_block, True), 4 * out_block, first_ortho
    )
    first_x = trade(first_ortho.reshape(4, ff_block, width), ("h", "m"))
    second_ortho = tie(second_ortho, first_x, first_g)
    second_x = trade(second_ortho.reshape(4, out_block, width), ("h", "m"))
    second_g = to_owner(tie(second_grad, first_ortho), quarter, second_ortho)


    grad_input = swap_halves(tie(grad_rows, first_ortho), my_h, my_x)

    head_count = gate_head.shape[0]
    small = sum_flips(tie(small_z, first_ortho), NEAR)
    small = sum_flips(tie(small, second_ortho), (("c",),))
    grad_gate = small[:head_count]
    grad_norm = small[head_count : head_count + 2]
    grad_head = small[head_count + 2, : 2 * head_dim].reshape(2, head_dim)
    new_mom_norm = 0.5 * mom_norm + 0.5 * grad_norm
    new_mom_head = 0.5 * mom_head + 0.5 * grad_head
    new_mom_gate = 0.5 * mom_gate_head + 0.5 * grad_gate
    new_norm = norm_gains - VECTOR_RATE * new_mom_norm
    new_head = head_gains - VECTOR_RATE * new_mom_head
    new_gate = gate_head.astype(F32) - VECTOR_RATE * new_mom_gate

    seq_len = tok_dev * n * 4
    out_boost = math.sqrt(width / max(1, 16384 // seq_len))
    rate = lambda rows: MATRIX_RATE * math.sqrt(rows * 8 * n)
    first_rates = {DOWN: rate(ff_block), GATE: rate(ff_block), UP: rate(ff_block)}
    second_rates = {
        QUERY: rate(out_block),
        OUT: out_boost * rate(out_block),
        KEY: rate(small_block),
        VALUE: rate(small_block),
    }
    q_at, k_at, v_at = 0, out_block, out_block + small_block
    o_at = v_at + small_block
    gate_at, up_at, down_at = (o_at + out_block + k * ff_block for k in range(3))
    g_gateup, g_down, m_gateup, m_down = settle(
        first_g, first_moms, first_moms, first_places, None
    )
    g_query, g_keyval, g_outproj, m_query, m_keyval, m_outproj = settle(
        second_g, second_moms, second_moms, second_places, None
    )
    n_gateup, n_down = settle(
        first_x,
        [old_rows],
        first_moms,
        (((GATE, gate_at), (UP, up_at)), ((DOWN, down_at),)),
        first_rates,
    )
    n_query, n_keyval, n_outproj = settle(
        second_x,
        [old_rows],
        second_moms,
        (((QUERY, q_at),), ((KEY, k_at), (VALUE, v_at)), ((OUT, o_at),)),
        second_rates,
    )

    return (
        output[None],
        grad_input[None],
        grad_norm,
        grad_head,
        grad_gate,
        g_query,
        g_keyval,
        g_outproj,
        g_gateup,
        g_down,
        new_mom_norm,
        new_mom_head,
        new_mom_gate,
        m_query,
        m_keyval,
        m_outproj,
        m_gateup,
        m_down,
        new_norm,
        new_head,
        new_gate,
        n_query,
        n_keyval,
        n_outproj,
        n_gateup,
        n_down,
    )


def solution(mesh):
    count = mesh.devices.size
    n = count // 8
    sizes = {"h": 2, "m": 2, "i": n // 4, "b": 2, "c": 2, "x": 2}
    fine = Mesh(mesh.devices.reshape(tuple(sizes[axis] for axis in ALL)), ALL)
    rows3 = P("x", CTX, None)
    own2 = P(ALL, None)
    own3 = P(None, ALL, None)
    half2 = P("x", None)
    half3 = P(None, "x", None)
    owners = (own2, own3, own2, own3, own2)
    return jax.shard_map(
        functools.partial(on_device, n),
        mesh=fine,
        in_specs=(rows3, rows3, P(), P(), P(), P(), half2, half3, half2, half3, half2)
        + (P(), P(), P())
        + owners,
        out_specs=(rows3, rows3, P(), P(), P())
        + owners
        + (P(), P(), P())
        + owners
        + (P(), P(), P())
        + owners,
        check_vma=False,
    )
```

time: 3340 us -> 596 us (0.18)
  waiting for transfers between devices: 2670 us -> 141 us
  matrix products: 353 us -> 26.6 us
  starting transfers between devices: 10.1 us -> 140 us
  Pallas kernels: 0 us -> 116 us
  blocking collectives: 67.6 us -> 0 us
  local copies, waits for them, and re-layouts: 119 us -> 67.2 us
    reduce_scatter x10 -> x1, waiting for transfers between devices: 1720 us -> 0.01 us  [on_device(): lax.psum_scatter(jnp.concatenate([grad_d, jnp.zeros_like(grad_d), grad_gu...]
    all_gather x14 -> x1, waiting for transfers between devices: 821 us -> 0.02 us  [on_device(): lax.all_gather(first_block, ('b', 'c', 'x'), axis=0, tiled=True)]
    dot_general x67 -> x12, matrix products: 353 us -> 26.6 us  [the longest x4 9.9 us: nt(): lax.dot_general(p, q, (((1,), (1,)), ((), ())), preferred_element_type=F32)]
    pallas_call x0 -> x36, Pallas kernels: none -> 116 us  [the longest x2 75 us: orthogonal(): pl.pallas_call(functools.partial(schulz_kernel, count), out_shape=jax.Sha...]
    psum x1 -> x0, waiting for transfers between devices: 105 us -> none  [on_device(): lax.psum((norm_terms, head_terms, grad_gate_head), ('ctx', 'wt'))]
    ppermute x0 -> x73, waiting for transfers between devices: none -> 97.3 us  [the longest x67 90.7 us: flip(): lax.ppermute(v, tuple(sorted(axes, key=ALL.index)), [(j, j ^ last) for j...]
    ppermute x0 -> x73, starting transfers between devices: none -> 95.3 us  [the longest x67 87.1 us: flip(): lax.ppermute(v, tuple(sorted(axes, key=ALL.index)), [(j, j ^ last) for j...]
    psum x1 -> x0, blocking collectives: 45.7 us -> none  [on_device(): lax.psum((norm_terms, head_terms, grad_gate_head), ('ctx', 'wt'))]
  transfers between devices with their start and end apart: 27 -> 85, of which waited for: 24 -> 30; matrix products, arithmetic and copies ran while one was open for 11% -> 20% of each run, Pallas kernels for 0% -> 18%
where the time goes in v1:
time: 596 us; the launch traced here: 586 us
  waiting for transfers between devices  141 us (24%)
  starting transfers between devices  140 us (23%)
  Pallas kernels  116 us (19%)
  other arithmetic  78.4 us (13%)
  local copies, waits for them, and re-layouts  67.2 us (11%)
  matrix products  26.6 us (4%)
  between operations  16.1 us (3%)
    ppermute x67, waiting for transfers between devices, flip(): lax.ppermute(v, tuple(sorted(axes, key=ALL.index)), [(j, j ^ last) for j...  90.7 us
    ppermute x67, starting transfers between devices, flip(): lax.ppermute(v, tuple(sorted(axes, key=ALL.index)), [(j, j ^ last) for j...  87.1 us
    pallas_call x2, Pallas kernels, orthogonal(): pl.pallas_call(functools.partial(schulz_kernel, count), out_shape=jax.Sha...  75 us
    all_to_all x10, starting transfers between devices, trade(): return lax.all_to_all(v, axes, split_axis=0, concat_axis=0, tiled=True)  44.9 us
    all_to_all x10, waiting for transfers between devices, trade(): return lax.all_to_all(v, axes, split_axis=0, concat_axis=0, tiled=True)  44.1 us
    unnamed x183, local copies, waits for them, and re-layouts  32 us
    pallas_call x1, Pallas kernels, attend_back(): pl.pallas_call(functools.partial(attend_back_kernel, scale), out_shape=(j...  15.2 us
  transfers between devices with their start and end apart: 85, of which 30 were waited for; matrix products, arithmetic and copies ran while one was open for 20% of the time, Pallas kernels for 18%

profile of v1, /device:TPU:0, one launch (start us, length us, event | category | flops | bytes accessed | tf_op | source)
XLA Modules:
  0.0 585.7 jit_solution(17770811647933072049)
XLA Ops:
  19.7 10.1 %collective-permute-start.3 = (bf16[128,1024]{1,0:T(8,128)(2,1)}, bf16[128,1024]{1,0:T(8,128)(2,1)S(1)}, u32[]{:S(2)}, u32[]{:S(2)}) collective-permute-start(bf16[128,1024]{1,0:T(8,128)(2,1)} %tie.19.refs_0_), channel_id=1, source_target_pairs={{0,5},{1,4},{4,1},{5,0},{2,7},{3,6},{6,3},{7,2},{8,13},{9,12},{12,... | collective-permute-start | bytes 786440 | tf_op jit(solution)/shard_map/ppermute | solution.py:39
  30.3 6.9 %collective-permute-done.3.refs_3_ = bf16[128,1024]{1,0:T(8,128)(2,1)S(1)} collective-permute-done((bf16[128,1024]{1,0:T(8,128)(2,1)}, bf16[128,1024]{1,0:T(8,128)(2,1)S(1)}, u32[]{:S(2)}, u32[]{:S(2)}) %collective-permute-start.3) | collective-permute-done | bytes 262176 | tf_op jit(solution)/shard_map/ppermute | solution.py:39
  63.3 5.0 collective-permute-done.8
  68.5 9.5 %attend.1 = f32[2048,256]{1,0:T(8,128)S(1)} custom-call(bf16[2048,128]{1,0:T(8,128)(2,1)S(1)} %pad_maximum_fusion.10.q_ref, bf16[2048,128]{1,0:T(8,128)(2,1)S(1)} %pad_maximum_fusion.11.k_ref, bf16[2048,256]{1,0:T(8,128)(2,1)S(1)} %concatenate.69.v_ref, s32[2048,1]{1,0:T(8,128)S(1)} %bitcast.145, s32[1,2048]{1,0:T(1,128)S(1)} %bitcast.147), custom_call_target="tpu_custom_call" | custom-call | flops 11811160064 | bytes 3145728 | tf_op jit(solution)/shard_map/attend/pallas_call | solution.py:357
  84.7 17.8 %collective-permute-start.28 = (bf16[128,1024]{1,0:T(8,128)(2,1)}, bf16[128,1024]{1,0:T(8,128)(2,1)S(1)}, u32[]{:S(2)}, u32[]{:S(2)}) collective-permute-start(bf16[128,1024]{1,0:T(8,128)(2,1)} %tie.20.refs_0_), channel_id=1, source_target_pairs={{0,5},{1,4},{4,1},{5,0},{2,7},{3,6},{6,3},{7,2},{8,13},{9,12},{12,... | collective-permute-start | bytes 786440 | tf_op jit(solution)/shard_map/ppermute | solution.py:39
  110.3 5.7 collective-permute-done.27.refs_2_
  115.9 4.6 collective-permute-start.26
  129.8 6.1 %collective-permute-done.16.refs_3_ = bf16[128,1024]{1,0:T(8,128)(2,1)S(1)} collective-permute-done((bf16[128,1024]{1,0:T(8,128)(2,1)S(1)}, bf16[128,1024]{1,0:T(8,128)(2,1)S(1)}, u32[]{:S(2)}, u32[]{:S(2)}) %collective-permute-start.16) | collective-permute-done | bytes 262176 | tf_op jit(solution)/shard_map/ppermute | solution.py:39
  165.6 6.3 %all-to-all-start.2 = ((bf16[4,96,1024]{2,1,0:T(8,128)(2,1)}), bf16[4,96,1024]{2,1,0:T(8,128)(2,1)}, u32[]{:S(2)}, u32[]{:S(2)}) async-start(bf16[4,96,1024]{2,1,0:T(8,128)(2,1)} %pack.3), calls=%async_computation.2 | async-start | bytes 1572864 | tf_op jit(solution)/shard_map/all_to_all | solution.py:115
  202.2 11.9 %all-to-all-done.2.refs_0_ = bf16[4,96,1024]{2,1,0:T(8,128)(2,1)} async-done(((bf16[4,96,1024]{2,1,0:T(8,128)(2,1)}), bf16[4,96,1024]{2,1,0:T(8,128)(2,1)}, u32[]{:S(2)}, u32[]{:S(2)}) %all-to-all-start.2) | async-done | bytes 786464 | tf_op jit(solution)/shard_map/all_to_all | solution.py:115
  236.3 5.1 all-to-all-done.refs_0_
  274.8 15.2 %attend_back.1 = (f32[2048,128]{1,0:T(8,128)S(1)}, f32[2048,128]{1,0:T(8,128)S(1)}, f32[2048,128]{1,0:T(8,128)S(1)}) custom-call(bf16[2048,128]{1,0:T(8,128)(2,1)S(1)} %copy-done.32, bf16[2048,128]{1,0:T(8,128)(2,1)S(1)} %copy-done.35, f32[1,2048]{1,0:T(1,128)S(1)} %div.80.cr_ref, s32[1,2048]{1,0:T(1,128)S(1)} %bitcast.150, ...), custom_call_target="tpu_custom_call" | custom-call | flops 21474836480 | bytes 4194304 | tf_op jit(solution)/shard_map/attend_back/pallas_call | solution.py:401
  317.9 6.6 %collective-permute-done.46 = bf16[256,1024]{1,0:T(8,128)(2,1)S(1)} collective-permute-done((bf16[256,1024]{1,0:T(8,128)(2,1)}, bf16[256,1024]{1,0:T(8,128)(2,1)S(1)}, u32[]{:S(2)}, u32[]{:S(2)}) %collective-permute-start.46) | collective-permute-done | bytes 524320 | tf_op jit(solution)/shard_map/ppermute | solution.py:746
  347.9 9.7 %collective-permute-start.53 = (bf16[128,1024]{1,0:T(8,128)(2,1)}, bf16[128,1024]{1,0:T(8,128)(2,1)S(1)}, u32[]{:S(2)}, u32[]{:S(2)}) collective-permute-start(bf16[128,1024]{1,0:T(8,128)(2,1)} %get-tuple-element.123), channel_id=1, source_target_pairs={{0,8},{8,0},{1,9},{9,1},{2,10},{10,2},{3,11},{11,3},{4,12},{12,4},... | collective-permute-start | bytes 786440 | tf_op jit(solution)/shard_map/ppermute | solution.py:39
  362.3 5.0 collective-permute-done.53
  371.3 17.7 %collective-permute-done.54 = bf16[128,1024]{1,0:T(8,128)(2,1)} collective-permute-done((bf16[128,1024]{1,0:T(8,128)(2,1)S(1)}, bf16[128,1024]{1,0:T(8,128)(2,1)}, u32[]{:S(2)}, u32[]{:S(2)}) %collective-permute-start.54) | collective-permute-done | bytes 262176 | tf_op jit(solution)/shard_map/ppermute | solution.py:39
  407.5 4.7 collective-permute-done.50
  412.2 4.3 collective-permute-done.52
  432.2 40.9 %schulz.2.refs_1_.refs_8_ = bf16[384,1024]{1,0:T(8,128)(2,1)} custom-call(s32[1,4]{1,0:T(1,128)S(1)} %add_bitcast_fusion.start_ref, bf16[3072,1024]{1,0:T(8,128)(2,1)} %all-gather.2.cloned.1.call-done.refs_0_, bf16[256,1024]{1,0:T(8,128)(2,1)S(1)} %bitcast.141), custom_call_target="tpu_custom_call" | custom-call | flops 47244640256 | bytes 12582912 | tf_op jit(solution)/shard_map/schulz/pallas_call | solution.py:546
  474.9 5.3 all-to-all-start.5
  498.5 5.8 all-to-all-start.7
  504.4 34.1 %schulz.3.refs_0_ = bf16[256,1024]{1,0:T(8,128)(2,1)S(1)} custom-call(s32[1,4]{1,0:T(1,128)S(1)} %add_bitcast_fusion.2.start_ref, bf16[256,1024]{1,0:T(8,128)(2,1)S(1)} %copy-done.9, bf16[256,1024]{1,0:T(8,128)(2,1)} %tie.30.refs_1_, bf16[256,1024]{1,0:T(8,128)(2,1)} %tie.31.refs_2_, bf16[256,1024]{1,0:T(8,128)(2,1)} %tie.32.refs_3_, ...), custom_call_target="tpu_custom_call" | custom-call | flops 47244640256 | bytes 8388608 | tf_op jit(solution)/shard_map/schulz/pallas_call | solution.py:546
  549.8 9.7 %all-to-all-done.9.items = bf16[4,64,1024]{2,1,0:T(8,128)(2,1)S(1)} async-done(((bf16[4,64,1024]{2,1,0:T(8,128)(2,1)}), bf16[4,64,1024]{2,1,0:T(8,128)(2,1)S(1)}, u32[]{:S(2)}, u32[]{:S(2)}) %all-to-all-start.9) | async-done | bytes 524320 | tf_op jit(solution)/shard_map/all_to_all | solution.py:115
  566.3 10.8 %all-to-all-done.8.items = bf16[4,64,1024]{2,1,0:T(8,128)(2,1)S(1)} async-done(((bf16[4,64,1024]{2,1,0:T(8,128)(2,1)}), bf16[4,64,1024]{2,1,0:T(8,128)(2,1)S(1)}, u32[]{:S(2)}, u32[]{:S(2)}) %all-to-all-start.8) | async-done | bytes 524320 | tf_op jit(solution)/shard_map/all_to_all | solution.py:115
  (511 shorter events, 310.9 us)
Async XLA Ops:
  7.2 250.1 %reduce-scatter.2.cloned.1.call-start = ((), (), s32[]{:S(2)}) async-start(), calls=%async_computation.11 | async-start | bytes 3932160 | tf_op jit(solution)/shard_map/reduce_scatter | solution.py:711
  81.8 22.4 %collective-permute-start.10 = (bf16[512,1024]{1,0:T(8,128)(2,1)}, bf16[512,1024]{1,0:T(8,128)(2,1)}, u32[]{:S(2)}, u32[]{:S(2)}) collective-permute-start(bf16[512,1024]{1,0:T(8,128)(2,1)} %slice.503), channel_id=1, source_target_pairs={{0,2},{2,0},{1,3},{3,1},{4,6},{6,4},{5,7},{7,5},{8,10},{10,8},{9,1... | collective-permute-start | bytes 3145736 | tf_op jit(solution)/shard_map/ppermute | solution.py:39
  84.7 25.5 %collective-permute-start.28 = (bf16[128,1024]{1,0:T(8,128)(2,1)}, bf16[128,1024]{1,0:T(8,128)(2,1)S(1)}, u32[]{:S(2)}, u32[]{:S(2)}) collective-permute-start(bf16[128,1024]{1,0:T(8,128)(2,1)} %tie.20.refs_0_), channel_id=1, source_target_pairs={{0,5},{1,4},{4,1},{5,0},{2,7},{3,6},{6,3},{7,2},{8,13},{9,12},{12,... | collective-permute-start | bytes 786440 | tf_op jit(solution)/shard_map/ppermute | solution.py:39
  162.9 25.2 %collective-permute-start.21 = (bf16[512,1024]{1,0:T(8,128)(2,1)}, bf16[512,1024]{1,0:T(8,128)(2,1)}, u32[]{:S(2)}, u32[]{:S(2)}) collective-permute-start(bf16[512,1024]{1,0:T(8,128)(2,1)} %slice.502), channel_id=1, source_target_pairs={{0,2},{2,0},{1,3},{3,1},{4,6},{6,4},{5,7},{7,5},{8,10},{10,8},{9,1... | collective-permute-start | bytes 3145736 | tf_op jit(solution)/shard_map/ppermute | solution.py:39
  165.6 48.5 %all-to-all-start.2 = ((bf16[4,96,1024]{2,1,0:T(8,128)(2,1)}), bf16[4,96,1024]{2,1,0:T(8,128)(2,1)}, u32[]{:S(2)}, u32[]{:S(2)}) async-start(bf16[4,96,1024]{2,1,0:T(8,128)(2,1)} %pack.3), calls=%async_computation.2 | async-start | bytes 1572864 | tf_op jit(solution)/shard_map/all_to_all | solution.py:115
  191.9 26.4 %collective-permute-start.22 = (bf16[128,1024]{1,0:T(8,128)(2,1)}, bf16[128,1024]{1,0:T(8,128)(2,1)}, u32[]{:S(2)}, u32[]{:S(2)}) collective-permute-start(bf16[128,1024]{1,0:T(8,128)(2,1)} %get-tuple-element.134), channel_id=1, source_target_pairs={{0,1},{1,0},{2,3},{3,2},{4,5},{5,4},{6,7},{7,6},{8,9},{9,8},{10,11... | collective-permute-start | bytes 786440 | tf_op jit(solution)/shard_map/ppermute | solution.py:39
  192.7 25.6 %collective-permute-start.24 = (bf16[128,1024]{1,0:T(8,128)(2,1)}, bf16[128,1024]{1,0:T(8,128)(2,1)}, u32[]{:S(2)}, u32[]{:S(2)}) collective-permute-start(bf16[128,1024]{1,0:T(8,128)(2,1)} %get-tuple-element.135), channel_id=1, source_target_pairs={{0,5},{1,4},{4,1},{5,0},{2,7},{3,6},{6,3},{7,2},{8,13},{9,12},{12,... | collective-permute-start | bytes 786440 | tf_op jit(solution)/shard_map/ppermute | solution.py:39
  193.8 24.5 %collective-permute-start.23 = (bf16[128,1024]{1,0:T(8,128)(2,1)}, bf16[128,1024]{1,0:T(8,128)(2,1)}, u32[]{:S(2)}, u32[]{:S(2)}) collective-permute-start(bf16[128,1024]{1,0:T(8,128)(2,1)} %get-tuple-element.136), channel_id=1, source_target_pairs={{0,4},{4,0},{1,5},{5,1},{2,6},{6,2},{3,7},{7,3},{8,12},{12,8},{9,1... | collective-permute-start | bytes 786440 | tf_op jit(solution)/shard_map/ppermute | solution.py:39
  214.1 27.3 %all-to-all-start = ((bf16[4,64,1024]{2,1,0:T(8,128)(2,1)}), bf16[4,64,1024]{2,1,0:T(8,128)(2,1)}, u32[]{:S(2)}, u32[]{:S(2)}) async-start(bf16[4,64,1024]{2,1,0:T(8,128)(2,1)} %copy-done.16), calls=%async_computation | async-start | bytes 1048576 | tf_op jit(solution)/shard_map/all_to_all | solution.py:115
  245.6 186.6 %all-gather.2.cloned.1.call-start = ((), (), s32[]{:S(2)}) async-start(), calls=%async_computation.12 | async-start | bytes 7077888 | tf_op jit(solution)/shard_map/all_gather | solution.py:811
  261.8 75.2 %all-to-all-start.1 = ((bf16[4,64,1024]{2,1,0:T(8,128)(2,1)}), bf16[4,64,1024]{2,1,0:T(8,128)(2,1)}, u32[]{:S(2)}, u32[]{:S(2)}) async-start(bf16[4,64,1024]{2,1,0:T(8,128)(2,1)} %pad_maximum_fusion.15), calls=%async_computation.1 | async-start | bytes 1048576 | tf_op jit(solution)/shard_map/all_to_all | solution.py:115
  305.1 25.1 %collective-permute-start.45 = (bf16[1024,128]{1,0:T(8,128)(2,1)S(1)}, bf16[1024,128]{1,0:T(8,128)(2,1)S(1)}, u32[]{:S(2)}, u32[]{:S(2)}) collective-permute-start(bf16[1024,128]{1,0:T(8,128)(2,1)S(1)} %slice.504), channel_id=1, source_target_pairs={{0,8},{8,0},{1,9},{9,1},{2,10},{10,2},{3,11},{11,3},{4,12},{12,4},... | collective-permute-start | bytes 786440 | tf_op jit(solution)/shard_map/ppermute | solution.py:39
  309.1 49.9 %collective-permute-start.56 = (bf16[480,1024]{1,0:T(8,128)(2,1)}, bf16[480,1024]{1,0:T(8,128)(2,1)}, u32[]{:S(2)}, u32[]{:S(2)}) collective-permute-start(bf16[480,1024]{1,0:T(8,128)(2,1)} %get-tuple-element.58), channel_id=1, source_target_pairs={{0,1},{1,0},{2,3},{3,2},{4,5},{5,4},{6,7},{7,6},{8,9},{9,8},{10,11... | collective-permute-start | bytes 2949128 | tf_op jit(solution)/shard_map/ppermute | solution.py:39
  341.8 52.6 %collective-permute-start.49 = (bf16[512,1024]{1,0:T(8,128)(2,1)}, bf16[512,1024]{1,0:T(8,128)(2,1)}, u32[]{:S(2)}, u32[]{:S(2)}) collective-permute-start(bf16[512,1024]{1,0:T(8,128)(2,1)} %slice.500), channel_id=1, source_target_pairs={{0,2},{2,0},{1,3},{3,1},{4,6},{6,4},{5,7},{7,5},{8,10},{10,8},{9,1... | collective-permute-start | bytes 3145736 | tf_op jit(solution)/shard_map/ppermute | solution.py:39
  358.0 31.0 %collective-permute-start.54 = (bf16[128,1024]{1,0:T(8,128)(2,1)S(1)}, bf16[128,1024]{1,0:T(8,128)(2,1)}, u32[]{:S(2)}, u32[]{:S(2)}) collective-permute-start(bf16[128,1024]{1,0:T(8,128)(2,1)S(1)} %get-tuple-element.125), channel_id=1, source_target_pairs={{0,16},{16,0},{1,17},{17,1},{2,18},{18,2},{3,19},{19,3},{4,20},{20... | collective-permute-start | bytes 786440 | tf_op jit(solution)/shard_map/ppermute | solution.py:39
  360.1 113.0 %collective-permute-start.48 = (bf16[128,1024]{1,0:T(8,128)(2,1)}, bf16[128,1024]{1,0:T(8,128)(2,1)}, u32[]{:S(2)}, u32[]{:S(2)}) collective-permute-start(bf16[128,1024]{1,0:T(8,128)(2,1)} %tie.24), channel_id=1, source_target_pairs={{1,16},{16,1},{3,18},{18,3},{5,20},{20,5},{7,22},{22,7},{9,24},{24... | collective-permute-start | bytes 786440 | tf_op jit(solution)/shard_map/ppermute | solution.py:107
  419.5 53.8 %collective-permute-start.60 = (f32[19,1024]{1,0:T(8,128)}, f32[19,1024]{1,0:T(8,128)S(1)}, u32[]{:S(2)}, u32[]{:S(2)}) collective-permute-start(f32[19,1024]{1,0:T(8,128)} %select_maximum_fusion), channel_id=1, source_target_pairs={{0,16},{16,0},{1,17},{17,1},{2,18},{18,2},{3,19},{19,3},{4,20},{20... | collective-permute-start | bytes 233480 | tf_op jit(solution)/shard_map/ppermute | solution.py:39
  419.5 62.5 %collective-permute-start.61 = (f32[19,1024]{1,0:T(8,128)}, f32[19,1024]{1,0:T(8,128)}, u32[]{:S(2)}, u32[]{:S(2)}) collective-permute-start(f32[19,1024]{1,0:T(8,128)} %select_maximum_fusion), channel_id=1, source_target_pairs={{0,24},{8,16},{16,8},{24,0},{1,25},{9,17},{17,9},{25,1},{2,26},{10... | collective-permute-start | bytes 233480 | tf_op jit(solution)/shard_map/ppermute | solution.py:39
  419.9 62.1 %collective-permute-start.59 = (f32[19,1024]{1,0:T(8,128)}, f32[19,1024]{1,0:T(8,128)}, u32[]{:S(2)}, u32[]{:S(2)}) collective-permute-start(f32[19,1024]{1,0:T(8,128)} %select_maximum_fusion), channel_id=1, source_target_pairs={{0,8},{8,0},{1,9},{9,1},{2,10},{10,2},{3,11},{11,3},{4,12},{12,4},... | collective-permute-start | bytes 233480 | tf_op jit(solution)/shard_map/ppermute | solution.py:39
  426.4 59.3 %collective-permute-start.67 = (bf16[256,1024]{1,0:T(8,128)(2,1)S(1)}, bf16[256,1024]{1,0:T(8,128)(2,1)}, u32[]{:S(2)}, u32[]{:S(2)}) collective-permute-start(bf16[256,1024]{1,0:T(8,128)(2,1)S(1)} %bitcast.140), channel_id=1, source_target_pairs={{0,5},{1,4},{4,1},{5,0},{2,7},{3,6},{6,3},{7,2},{8,13},{9,12},{12,... | collective-permute-start | bytes 1572872 | tf_op jit(solution)/shard_map/ppermute | solution.py:39
  428.4 46.5 %all-to-all-start.6 = ((bf16[4,96,1024]{2,1,0:T(8,128)(2,1)}), bf16[4,96,1024]{2,1,0:T(8,128)(2,1)S(1)}, u32[]{:S(2)}, u32[]{:S(2)}) async-start(bf16[4,96,1024]{2,1,0:T(8,128)(2,1)} %tie.33), calls=%async_computation.7 | async-start | bytes 1572864 | tf_op jit(solution)/shard_map/all_to_all | solution.py:115
  474.9 23.6 %all-to-all-start.5 = ((bf16[4,96,1024]{2,1,0:T(8,128)(2,1)}), bf16[4,96,1024]{2,1,0:T(8,128)(2,1)S(1)}, u32[]{:S(2)}, u32[]{:S(2)}) async-start(bf16[4,96,1024]{2,1,0:T(8,128)(2,1)} %bitcast.63), calls=%async_computation.6 | async-start | bytes 1572864 | tf_op jit(solution)/shard_map/all_to_all | solution.py:115
  495.3 51.3 %collective-permute-start.58 = (f32[128,1024]{1,0:T(8,128)}, f32[128,1024]{1,0:T(8,128)}, u32[]{:S(2)}, u32[]{:S(2)}) collective-permute-start(f32[128,1024]{1,0:T(8,128)} %tie.27), channel_id=1, source_target_pairs={{1,16},{16,1},{3,18},{18,3},{5,20},{20,5},{7,22},{22,7},{9,24},{24... | collective-permute-start | bytes 1572872 | tf_op jit(solution)/shard_map/ppermute | solution.py:107
  498.5 40.8 %all-to-all-start.7 = ((bf16[4,64,1024]{2,1,0:T(8,128)(2,1)}), bf16[4,64,1024]{2,1,0:T(8,128)(2,1)S(1)}, u32[]{:S(2)}, u32[]{:S(2)}) async-start(bf16[4,64,1024]{2,1,0:T(8,128)(2,1)} %tie.36), calls=%async_computation.8 | async-start | bytes 1048576 | tf_op jit(solution)/shard_map/all_to_all | solution.py:115
  (150 other events, 1393.5 us)
Sparse Core Ops, SparseCore 0:
  152.0 79.1 reduce-scatter.1
  260.0 47.8 all-gather.1

commit v2 on v1

--- a/solution.py
+++ b/solution.py
@@ -121,19 +121,6 @@
 
 def fold_pairs(q):
     return [(i * 2 + b, b * q + i) for i in range(q) for b in range(2)]
-
-
-def to_home(items, q, token):
-    if q > 1:
-        items = lax.ppermute(items, ("i", "b"), [(d, s) for s, d in fold_pairs(q)])
-    return trade(turned(tie(trade(items, ("h", "m")), token)), ("c", "x"))
-
-
-def to_owner(blocks, q, token):
-    items = trade(tie(turned(trade(blocks, ("c", "x"))), token), ("h", "m"))
-    if q > 1:
-        items = lax.ppermute(items, ("i", "b"), fold_pairs(q))
-    return items
 
 
 VMEM_SPEC = pl.BlockSpec(memory_space=pltpu.VMEM)
@@ -251,19 +238,12 @@
 
 def pack_kernel(places, ins, *refs):
     out = refs[-1]
-    height, width = out.shape[1:]
-    filled = set()
+    out[...] = jnp.zeros_like(out)
     for ref, item in zip(refs[:ins], places):
         rows = ref.shape[-2]
-        for j, member in enumerate(item):
+        for j, (member, first) in enumerate(item):
             source = ref[j] if len(ref.shape) == 3 else ref[...]
-            out[member, :rows] = source.astype(BF16)
-            if rows < height:
-                out[member, rows:] = jnp.zeros((height - rows, width), BF16)
-            filled.add(member)
-    for member in range(4):
-        if member not in filled:
-            out[member] = jnp.zeros((height, width), BF16)
+            out[member, first : first + rows] = source.astype(BF16)
 
 
 def pack(arrays, places, height, *tokens):
@@ -330,105 +310,262 @@
 
 
 TILE = 512
-
-
-def tile_at(j):
-    return pl.ds(pl.multiple_of(j * TILE, TILE), TILE)
-
-
-def attend_kernel(scale, q_ref, k_ref, v_ref, qp_ref, kp_ref, o_ref):
-    @pl.loop(0, q_ref.shape[0] // TILE)
-    def _(i):
-        query, place = q_ref[tile_at(i), :], qp_ref[tile_at(i), :]
-
-        def step(j, acc):
-            scores = nt(query, k_ref[tile_at(j), :])
-            weights = jnp.where(kp_ref[:, tile_at(j)] <= place, jnp.exp2(scores * scale), 0.0)
-            return acc + nn(weights.astype(BF16), v_ref[tile_at(j), :])
-
-        o_ref[tile_at(i), :] = lax.fori_loop(
-            0, k_ref.shape[0] // TILE, step, jnp.zeros((TILE, v_ref.shape[1]), F32)
+ATTENTION = pltpu.CompilerParams(vmem_limit_bytes=44 * 2**20)
+
+
+def tile_at(j, size=TILE, offset=0):
+    return pl.ds(pl.multiple_of(j * size + offset, size), size)
+
+
+def shape_of(dtype, *shape):
+    return jax.ShapeDtypeStruct(shape, dtype)
+
+
+def cost(microseconds):
+    return pl.CostEstimate(
+        flops=int(microseconds * 1.15e9), bytes_accessed=2**20, transcendentals=0
+    )
+
+
+def head_scale(raw):
+    return lax.rsqrt(jnp.mean(raw * raw, axis=-1, keepdims=True) + NORM_EPS)
+
+
+def head_back(grad, raw, cosine, sine, gain):
+    grad = grad * cosine - pltpu.roll(grad, grad.shape[1] // 2, 1) * sine
+    scale = head_scale(raw)
+    unit = raw * scale
+    pushed = grad * gain
+    back = scale * (pushed - unit * jnp.mean(pushed * unit, axis=-1, keepdims=True))
+    return back, jnp.sum(grad * unit, axis=0, keepdims=True)
+
+
+def project_kernel(heads, n_ref, w_ref, cos_ref, sin_ref, gain_ref, q_ref, kv_ref, lg_ref, raw_ref):
+    rows, dim = n_ref.shape[0], cos_ref.shape[1]
+
+    @pl.loop(0, rows // 256)
+    def _(t):
+        span = tile_at(t, 256)
+        out = nt(n_ref[span, :], w_ref[...])
+        cosine, sine = cos_ref[span, :], sin_ref[span, :]
+        for j in range(heads + 1):
+            raw = out[:, j * dim : (j + 1) * dim]
+            raw_ref[j, span, :] = raw
+            which = slice(0, 1) if j < heads else slice(1, 2)
+            unit = raw * head_scale(raw) * gain_ref[which, :]
+            turned_rows = unit * cosine + pltpu.roll(unit, dim // 2, 1) * sine
+            if j < heads:
+                q_ref[j, span, :] = turned_rows.astype(BF16)
+            else:
+                kv_ref[0, span, :] = turned_rows.astype(BF16)
+        kv_ref[1, span, :] = out[:, (heads + 1) * dim : (heads + 2) * dim].astype(BF16)
+        lg_ref[span, :] = jax.nn.sigmoid(out[:, (heads + 2) * dim : (heads + 3) * dim])
+
+
+def project(normed, w_in, cosine, sine, gains):
+    rows, dim = cosine.shape
+    heads = w_in.shape[0] // dim - 3
+    return pl.pallas_call(
+        functools.partial(project_kernel, heads),
+        out_shape=[
+            shape_of(BF16, heads, rows, dim),
+            shape_of(BF16, 2, rows, dim),
+            shape_of(F32, rows, dim),
+            shape_of(F32, heads + 1, rows, dim),
+        ],
+        in_specs=[VMEM_SPEC] * 5,
+        out_specs=[VMEM_SPEC] * 4,
+        compiler_params=ATTENTION,
+        cost_estimate=cost(6),
+        name="project",
+    )(normed, w_in, cosine, sine, gains)
+
+
+def widened(values):
+    return jnp.concatenate([values, jnp.ones_like(values)], axis=1)
+
+
+def attend_kernel(scale, q_ref, lg_ref, qp_ref, kp_ref, *refs):
+    pieces, (att_ref, tot_ref, gated_ref) = refs[:-3], refs[-3:]
+    heads, rows, dim = q_ref.shape
+    for h in range(heads):
+
+        @pl.loop(0, rows // TILE)
+        def _(i):
+            span = tile_at(i)
+            query, place = q_ref[h, span, :], qp_ref[span, :]
+            total = jnp.zeros((TILE, 2 * dim), F32)
+            for number, kv_ref in enumerate(pieces):
+                offset = number * kv_ref.shape[1]
+
+                def step(j, acc, kv_ref=kv_ref, offset=offset):
+                    scores = nt(query, kv_ref[0, tile_at(j), :])
+                    seen = kp_ref[:, tile_at(j, offset=offset)] <= place
+                    weights = jnp.where(seen, jnp.exp2(scores * scale), 0.0)
+                    return acc + nn(weights.astype(BF16), widened(kv_ref[1, tile_at(j), :]))
+
+                total = lax.fori_loop(0, kv_ref.shape[1] // TILE, step, total)
+            weight = total[:, dim : dim + 1]
+            attended = total[:, :dim] / weight
+            att_ref[h, span, :] = attended
+            tot_ref[h, span, :] = weight
+            gated_ref[span, h * dim : (h + 1) * dim] = (
+                attended * lg_ref[span, h : h + 1]
+            ).astype(BF16)
+
+
+def attend(query, sigmoids, pieces, q_place, k_place, scale, *tokens):
+    heads, rows, dim = query.shape
+    count = len(pieces)
+    kernel = functools.partial(attend_kernel, scale * math.log2(math.e))
+
+    def without_tokens(*refs):
+        kernel(*refs[: 4 + count], *refs[4 + count + len(tokens) :])
+
+    return pl.pallas_call(
+        without_tokens,
+        out_shape=[
+            shape_of(F32, heads, rows, dim),
+            shape_of(F32, heads, rows, 1),
+            shape_of(BF16, rows, heads * dim),
+        ],
+        in_specs=[VMEM_SPEC] * (4 + count) + [HBM_SPEC] * len(tokens),
+        out_specs=[VMEM_SPEC] * 3,
+        compiler_params=ATTENTION,
+        cost_estimate=cost(12),
+        name="attend",
+    )(query, sigmoids, q_place[:, None], k_place[None, :], *pieces, *tokens)
+
+
+def before_kernel(b_ref, w_ref, att_ref, tot_ref, lg_ref, bw_ref, dl_ref):
+    heads, rows, dim = att_ref.shape
+    lanes = lax.broadcasted_iota(jnp.int32, (256, dim), 1)
+
+    @pl.loop(0, rows // 256)
+    def _(t):
+        span = tile_at(t, 256)
+        grad = nt(b_ref[span, :], w_ref[...])
+        logits = jnp.zeros((256, dim), F32)
+        for h in range(heads):
+            part = grad[:, h * dim : (h + 1) * dim]
+            sig = lg_ref[span, h : h + 1]
+            total = tot_ref[h, span, :]
+            along = jnp.sum(part * att_ref[h, span, :], axis=-1, keepdims=True)
+            logits = jnp.where(lanes == h, sig * (1.0 - sig) * along, logits)
+            bw_ref[h, span, :dim] = (part * (sig / total)).astype(BF16)
+            corr = -sig * along / total
+            high = corr.astype(BF16).astype(F32)
+            extra = jnp.where(lanes == 0, high, jnp.where(lanes == 1, corr - high, 0.0))
+            bw_ref[h, span, dim:] = extra.astype(BF16)
+        dl_ref[span, :] = logits.astype(BF16)
+
+
+def before_attention(dbranch, wo, attended, total, sigmoids):
+    heads, rows, dim = attended.shape
+    return pl.pallas_call(
+        before_kernel,
+        out_shape=[shape_of(BF16, heads, rows, 2 * dim), shape_of(BF16, rows, dim)],
+        in_specs=[VMEM_SPEC] * 5,
+        out_specs=[VMEM_SPEC] * 2,
+        compiler_params=ATTENTION,
+        cost_estimate=cost(5),
+        name="before",
+    )(dbranch, wo, attended, total, sigmoids)
+
+
+def attend_back_kernel(
+    scale, count, q_ref, bw_ref, raw_ref, cos_ref, sin_ref, gain_ref, qp_ref, kp_ref, *refs
+):
+    pieces = refs[:count]
+    dq_ref, terms_ref = refs[count : count + 2]
+    outs, sums = refs[count + 2 : 2 * count + 2], refs[2 * count + 2 :]
+    heads, rows, dim = q_ref.shape
+    grow = scale * math.log2(math.e)
+    for ref in sums:
+        ref[...] = jnp.zeros_like(ref)
+    terms_ref[...] = jnp.zeros_like(terms_ref)
+    for h in range(heads):
+
+        @pl.loop(0, rows // TILE)
+        def _(i):
+            span = tile_at(i)
+            query, back, place = q_ref[h, span, :], bw_ref[h, span, :], qp_ref[:, span]
+            total = jnp.zeros((TILE, dim), F32)
+            for number, (kv_ref, sum_ref) in enumerate(zip(pieces, sums)):
+                offset = number * kv_ref.shape[1]
+
+                def step(j, acc, kv_ref=kv_ref, sum_ref=sum_ref, offset=offset):
+                    keys = tile_at(j)
+                    key = kv_ref[0, keys, :]
+                    seen = kp_ref[tile_at(j, offset=offset), :] <= place
+                    weights = jnp.where(seen, jnp.exp2(nt(key, query) * grow), 0.0)
+                    push = nt(widened(kv_ref[1, keys, :]), back)
+                    dscore = (weights * push * scale).astype(BF16)
+                    sum_ref[1, keys, :] += nn(weights.astype(BF16), back[:, :dim])
+                    sum_ref[0, keys, :] += nn(dscore, query)
+                    return acc + tn(dscore, key)
+
+                total = lax.fori_loop(0, kv_ref.shape[1] // TILE, step, total)
+            grad, terms = head_back(
+                total, raw_ref[h, span, :], cos_ref[span, :], sin_ref[span, :], gain_ref[0:1, :]
+            )
+            dq_ref[span, h * dim : (h + 1) * dim] = grad.astype(BF16)
+            terms_ref[...] += terms
+
+    for out, ref in zip(outs, sums):
+        out[...] = ref[...].astype(out.dtype)
+
+
+def attend_back(query, back, raw, cosine, sine, gains, pieces, q_place, k_place, scale):
+    heads, rows, dim = query.shape
+    count = len(pieces)
+    return pl.pallas_call(
+        functools.partial(attend_back_kernel, scale, count),
+        out_shape=[shape_of(BF16, rows, heads * dim), shape_of(F32, 1, dim)]
+        + [shape_of(BF16 if k else F32, *piece.shape) for k, piece in enumerate(pieces)],
+        in_specs=[VMEM_SPEC] * (8 + count),
+        out_specs=[VMEM_SPEC] * (2 + count),
+        scratch_shapes=[pltpu.VMEM(piece.shape, F32) for piece in pieces],
+        compiler_params=ATTENTION,
+        cost_estimate=cost(18),
+        name="attend_back",
+    )(
+        query, back, raw, cosine, sine, gains, q_place[None, :], k_place[:, None], *pieces
+    )
+
+
+def keys_kernel(own_ref, far_ref, raw_ref, cos_ref, sin_ref, gain_ref, dl_ref, out_ref, terms_ref):
+    rows, dim = cos_ref.shape
+    terms_ref[...] = jnp.zeros_like(terms_ref)
+
+    @pl.loop(0, rows // 256)
+    def _(t):
+        span = tile_at(t, 256)
+        both = [own_ref[k, span, :] + far_ref[k, span, :].astype(F32) for k in range(2)]
+        grad, terms = head_back(
+            both[0], raw_ref[raw_ref.shape[0] - 1, span, :], cos_ref[span, :], sin_ref[span, :], gain_ref[1:2, :]
         )
-
-
-def attend(query, key, wide, q_place, k_place, scale):
-    rows, dim = query.shape
-    keys = key.shape[0]
-    out = pl.pallas_call(
-        functools.partial(attend_kernel, scale * math.log2(math.e)),
-        out_shape=jax.ShapeDtypeStruct((rows, 2 * dim), F32),
-        in_specs=[VMEM_SPEC] * 5,
-        out_specs=VMEM_SPEC,
-        compiler_params=pltpu.CompilerParams(vmem_limit_bytes=40 * 2**20),
-        cost_estimate=pl.CostEstimate(
-            flops=22 * rows * keys * dim, bytes_accessed=rows * dim * 12, transcendentals=0
-        ),
-        name="attend",
-    )(query, key, wide, q_place[:, None], k_place[None, :])
-    return out[:, :dim], out[:, dim : dim + 1]
-
-
-def attend_back_kernel(
-    scale, q_ref, w_ref, cr_ref, qp_ref, k_ref, v_ref, kp_ref, dq_ref, dk_ref, dv_ref
-):
-    dk_ref[...] = jnp.zeros_like(dk_ref)
-    dv_ref[...] = jnp.zeros_like(dv_ref)
-    grow = scale * math.log2(math.e)
-
-    @pl.loop(0, q_ref.shape[0] // TILE)
-    def _(i):
-        query, back = q_ref[tile_at(i), :], w_ref[tile_at(i), :]
-        place, corr = qp_ref[:, tile_at(i)], cr_ref[:, tile_at(i)]
-
-        def step(j, acc):
-            span = tile_at(j)
-            key = k_ref[span, :]
-            weights = jnp.where(kp_ref[span, :] <= place, jnp.exp2(nt(key, query) * grow), 0.0)
-            push = nt(v_ref[span, :], back)
-            dscore = (weights * (push - corr) * scale).astype(BF16)
-            dv_ref[span, :] += nn(weights.astype(BF16), back)
-            dk_ref[span, :] += nn(dscore, query)
-            return acc + tn(dscore, key)
-
-        dq_ref[tile_at(i), :] = lax.fori_loop(
-            0, k_ref.shape[0] // TILE, step, jnp.zeros(query.shape, F32)
-        )
-
-
-def attend_back(query, back, corr, key, value, q_place, k_place, scale):
-    rows, dim = query.shape
-    keys = key.shape[0]
-    return pl.pallas_call(
-        functools.partial(attend_back_kernel, scale),
-        out_shape=(
-            jax.ShapeDtypeStruct((rows, dim), F32),
-            jax.ShapeDtypeStruct((keys, dim), F32),
-            jax.ShapeDtypeStruct((keys, dim), F32),
-        ),
+        terms_ref[...] += terms
+        out_ref[span, :dim] = grad.astype(BF16)
+        out_ref[span, dim : 2 * dim] = both[1].astype(BF16)
+        out_ref[span, 2 * dim :] = dl_ref[span, :]
+
+
+def keys_back(own, far, raw, cosine, sine, gains, dlogit):
+    rows, dim = cosine.shape
+    return pl.pallas_call(
+        keys_kernel,
+        out_shape=[shape_of(BF16, rows, 3 * dim), shape_of(F32, 1, dim)],
         in_specs=[VMEM_SPEC] * 7,
-        out_specs=[VMEM_SPEC] * 3,
-        compiler_params=pltpu.CompilerParams(vmem_limit_bytes=40 * 2**20),
-        cost_estimate=pl.CostEstimate(
-            flops=40 * rows * keys * dim, bytes_accessed=rows * dim * 16, transcendentals=0
-        ),
-        name="attend_back",
-    )(query, back, corr[None, :], q_place[None, :], key, value, k_place[:, None])
+        out_specs=[VMEM_SPEC] * 2,
+        compiler_params=ATTENTION,
+        cost_estimate=cost(3),
+        name="keys",
+    )(own, far, raw, cosine, sine, gains, dlogit)
 
 
 def rms_scale(v):
     return lax.rsqrt(jnp.mean(v * v, axis=-1, keepdims=True) + NORM_EPS)
-
-
-def rotate(v, cosine, sine):
-    half = v.shape[-1] // 2
-    lead, trail = v[..., :half], v[..., half:]
-    return jnp.concatenate([lead * cosine - trail * sine, trail * cosine + lead * sine], axis=-1)
-
-
-def rotate_back(g, cosine, sine):
-    half = g.shape[-1] // 2
-    lead, trail = g[..., :half], g[..., half:]
-    return jnp.concatenate([lead * cosine + trail * sine, trail * cosine - lead * sine], axis=-1)
 
 
 def norm_back(grad, scaled, rscale, gains):
@@ -524,10 +661,7 @@
     inv = 1.0 / (jnp.sqrt(square) + 1e-07)
     first = square * inv * inv * (1.0 / width)
     settle_gram(inv * inv, first)
-    rows = own // 4
-    for k in range(4):
-        block = x_ref[pl.ds(pl.multiple_of(start_ref[0, k], rows), rows), :]
-        x_own[k * rows : (k + 1) * rows, :] = block.astype(F32) * inv
+    x_own[...] = x_ref[pl.ds(pl.multiple_of(start_ref[0, 0], own), own), :].astype(F32) * inv
 
     def sweep(_, d):
         p = make_poly(d)
@@ -649,44 +783,49 @@
     else:
         key_place = jnp.concatenate([group_place(r) for r in range(n // 2)])
 
-    def gather_keys(v):
+    def key_pieces(kv):
         if n == 4:
-            return jnp.concatenate([v, flip(v, "m")], axis=0)
-        return lax.all_gather(v, ("m", "i"), axis=0, tiled=True)
-
-    def sum_keys(v):
+            return [kv, flip(kv, "m")]
+        return [lax.all_gather(kv, ("m", "i"), axis=1, tiled=True)]
+
+    def key_sums(parts):
         if n == 4:
-            return v[:group_rows] + flip(v[group_rows:].astype(BF16), "m").astype(F32)
-        return lax.psum_scatter(v, ("m", "i"), scatter_dimension=0, tiled=True)
-
-    inverse = ROPE_BASE ** (-(2.0 * jnp.arange(head_dim // 2, dtype=F32)) / head_dim)
+            return parts[0], flip(parts[1], "m")
+        mine = lax.psum_scatter(parts[0], ("m", "i"), scatter_dimension=1, tiled=True)
+        return mine, jnp.zeros(mine.shape, BF16)
+
+    half = head_dim // 2
+    inverse = ROPE_BASE ** (-(2.0 * jnp.arange(half, dtype=F32)) / head_dim)
     angles = place.astype(F32)[:, None] * inverse[None, :]
     cosine, sine = jnp.cos(angles), jnp.sin(angles)
-    normed_rows = tie(normed_rows, w_in, cosine, key_place)
+    cosine = jnp.concatenate([cosine, cosine], axis=1)
+    sine = jnp.concatenate([-sine, sine], axis=1)
+    normed_rows = tie(normed_rows, w_in, cosine, sine, key_place)
     normed = gather_group(normed_rows)
-    projected = nt(normed, w_in)
-    rows_cot = swap_halves(held(cotangent[0], normed_rows), my_h, my_x)
-    cot_near = gather_near(tie(rows_cot, projected))
-    query_raw = jnp.stack(
-        [projected[:, j * head_dim : (j + 1) * head_dim] for j in range(heads_here)]
-    )
-    key_raw = projected[:, q_rows : q_rows + kv_rows]
-    value_rows = projected[:, q_rows + kv_rows : q_rows + 2 * kv_rows].astype(BF16)
-    logits = projected[:, q_rows + 2 * kv_rows : q_rows + 2 * kv_rows + heads_here]
-    rq, rk = rms_scale(query_raw), rms_scale(key_raw)
-    yq, yk = query_raw * rq, key_raw * rk
-    query_rows = rotate(yq * head_gains[0], cosine, sine).astype(BF16)
-    key_rows = rotate(yk * head_gains[1], cosine, sine).astype(BF16)
-    key_all, value_all = gather_keys(key_rows), gather_keys(value_rows)
-    flat_query = query_rows.reshape(heads_here * group_rows, head_dim)
-    flat_place = jnp.tile(place, heads_here)
-    wide = jnp.concatenate([value_all, jnp.ones_like(value_all)], axis=1)
-    summed, total = attend(flat_query, key_all, wide, flat_place, key_place, scale)
-    attended = (summed / total).reshape(heads_here, group_rows, head_dim)
-    total = total.reshape(heads_here, group_rows, 1)
-    gate_sig = jax.nn.sigmoid(logits).T[:, :, None]
-    gated = attended * gate_sig
-    gated = jnp.concatenate([gated[j] for j in range(heads_here)], axis=1).astype(BF16)
+    query_rows, kv_rows_here, sigmoids, raw = project(normed, w_in, cosine, sine, head_gains)
+    rows_cot = swap_halves(held(cotangent[0], w_in, cosine), my_h, my_x)
+    kv_all = key_pieces(kv_rows_here)
+    cot_near = gather_near(tie(rows_cot, query_rows))
+    attended, total, gated = attend(
+        query_rows, sigmoids, kv_all, place, key_place, scale, rows_cot
+    )
+    gated = tie(gated, *cot_near)
+
+    first_moms = (mom_gateup, mom_down)
+    first_places = ((GATE, UP), (DOWN,))
+    second_moms = (mom_query, mom_keyval, mom_outproj)
+    second_places = ((QUERY,), (KEY, VALUE), (OUT,))
+    old_items = pack(
+        first_moms + second_moms,
+        [[(member, 0) for member in place] for place in first_places]
+        + [[(member, ff_block) for member in place] for place in second_places],
+        ff_block + out_block,
+        query_rows,
+    )
+    if quarter > 1:
+        old_items = lax.ppermute(old_items, ("i", "b"), [(d, p) for p, d in fold_pairs(quarter)])
+    old_items = trade(old_items, ("h", "m"))
+
     middle = xf + sum_group(nn(gated, wo))
     grad_all = gather_far(cot_near)
     r2 = rms_scale(middle)
@@ -706,6 +845,7 @@
         ],
         axis=1,
     )
+    dgu = tie(dgu, old_items)
     grad_gu = tn(dgu, hidden_in).astype(BF16)
     grad_d = tn(hidden, grad_all).astype(BF16)
     ff_grad = lax.psum_scatter(
@@ -718,44 +858,13 @@
     gout = rows_cot.astype(F32)
     norm_terms_mid = jnp.sum(dhn * y2, axis=0)
     dmiddle = gout + norm_back(dhn, y2, r2, norm_gains[1])
-    dbranch = gather_group(dmiddle.astype(BF16))
-
-    first_moms = (mom_gateup, mom_down)
-    first_places = ((GATE, UP), (DOWN,))
-    second_moms = (mom_query, mom_keyval, mom_outproj)
-    second_places = ((QUERY,), (KEY, VALUE), (OUT,))
-    first_pack = pack(first_moms, first_places, ff_block, middle)
-    second_pack = pack(second_moms, second_places, out_block, gate_up)
-    first_old = to_home(first_pack, quarter, dhn)
-    second_old = to_home(second_pack, quarter, dbranch)
-
-    spot = me % (4 * n)
-    mine_now, other_now = owned_rows(
-        jnp.stack([spot, spot ^ 1]).reshape(1, 2),
-        (w_query, w_keyval, w_outproj, w_gateup, w_down),
-        n,
-        dbranch,
-    )
-    old_rows = jnp.where(my_x == my_h, mine_now, flip(other_now, "x"))
-
-    dgated = nt(dbranch, wo)
+    out_sum = sum_core(nn(hidden, wd))
+    dbranch = gather_group(tie(dmiddle.astype(BF16), out_sum))
+
+    back_w, dlogit = before_attention(dbranch, wo, attended, total, sigmoids)
+
     def over_i(v):
         return lax.psum_scatter(v, "i", scatter_dimension=0, tiled=True) if quarter > 1 else v
-
-    def to_out_plane(v):
-        v = v.astype(F32) + lax.ppermute(v, ("h", "m"), [(0, 1), (3, 2)]).astype(F32)
-        return v + lax.ppermute(v.astype(BF16), ("h", "m"), [(2, 1)]).astype(F32)
-
-    def to_block(v):
-        v = v.reshape(-1, width)
-        return jnp.concatenate(
-            [v]
-            + [
-                lax.ppermute(v, "i", [((j + d) % quarter, j) for j in range(quarter)])
-                for d in range(1, quarter)
-            ],
-            axis=0,
-        )
 
     def blend(old, grad):
         return (0.5 * old.astype(F32) + 0.5 * grad.astype(F32)).astype(BF16)
@@ -764,89 +873,53 @@
         blocks = v.reshape(4, rows, width)
         return jnp.pad(blocks, ((0, 0), (0, height - rows), (0, 0)))
 
-    position = my_b * 1 + my_i * 2
-    source_b, source_i = position // quarter, position % quarter
-
-    def firsts(rows, mine_first):
-        return jnp.stack(
-            [
-                (
-                    (((my_c ^ m) * 2 + (source_b ^ my_b)) * 2 + (my_x ^ h))
-                    if mine_first
-                    else (source_b * 2 + m) * 2 + h
-                )
-                * (4 * quarter * rows)
-                + ((source_i - my_i) % quarter) * (4 * rows)
-                + (my_c * 2 + my_x) * rows
-                for h in range(2)
-                for m in range(2)
-            ]
-        ).reshape(1, 4)
-
-    grad_o = to_out_plane(over_i(tn(gated, dbranch).astype(BF16)))
+    everyone = ("i", "b", "c", "x")
+    mine_at = lax.axis_index(everyone)
+
+    grad_o = over_i(tn(gated, dbranch).astype(BF16))
+    grad_o = grad_o.astype(F32) + lax.ppermute(grad_o, ("h", "m"), [(0, 1), (3, 2)]).astype(F32)
     first_grad = ff_grad.reshape(4, ff_block, width)
-    first_mine = blend(first_old, first_grad)
-    out_sum = sum_core(nn(hidden, wd))
-
-    dgated = jnp.stack([dgated[:, j * head_dim : (j + 1) * head_dim] for j in range(heads_here)])
-    dattended = dgated * gate_sig
-    dlogit = (
-        gate_sig * (1.0 - gate_sig) * jnp.sum(dgated * attended, axis=-1, keepdims=True)
-    ).astype(BF16)
-    corr = jnp.sum(dattended * attended, axis=-1, keepdims=True) / total
-    back_w = (dattended / total).astype(BF16)
-    dquery, dkey_part, dvalue_part = attend_back(
-        flat_query,
-        back_w.reshape(heads_here * group_rows, head_dim),
-        corr.reshape(heads_here * group_rows),
-        key_all,
-        value_all,
-        flat_place,
-        key_place,
-        scale,
+    out_sum = tie(out_sum, back_w)
+
+    dq, query_terms, *kv_sums = attend_back(
+        query_rows, back_w, raw, cosine, sine, head_gains, kv_all, place, key_place, scale
     )
     out_rows = middle + sum_near(out_sum)
-    dkey_part = tie(dkey_part, out_rows)
-    first_block = to_block(first_mine)
-    first_start = lax.all_gather(first_block, ("b", "c", "x"), axis=0, tiled=True)
-    dkey, dvalue = sum_keys(dkey_part), sum_keys(dvalue_part)
-    dqn = rotate_back(dquery.reshape(heads_here, group_rows, head_dim), cosine, sine)
-    dkn = rotate_back(dkey, cosine, sine)
-    head_terms = jnp.stack([jnp.sum(dqn * yq, axis=(0, 1)), jnp.sum(dkn * yk, axis=0)])
-    dq = norm_back(dqn, yq, rq, head_gains[0]).astype(BF16)
-    dk = norm_back(dkn, yk, rk, head_gains[1]).astype(BF16)
-    dall = jnp.concatenate(
-        [dq[j] for j in range(heads_here)]
-        + [dk, dvalue.astype(BF16)]
-        + [dlogit[j] for j in range(heads_here)]
-        + [jnp.zeros((group_rows, gate_pad), BF16)],
-        axis=1,
-    )
-    dall = tie(dall, second_old, grad_o)
-    grad_in = tn(dall, normed)
-    query_part = grad_in[:q_rows].reshape(n, 2, small_block, width)
+    first_mid = turned(trade(tie(first_grad, dq), ("c", "x")))
+    kv_sums[0] = tie(kv_sums[0], out_rows)
+    first_old, second_old = old_items[:, :ff_block], old_items[:, ff_block:]
+    first_block = blend(first_old, first_mid).reshape(4 * ff_block, width)
+    first_start = lax.all_gather(first_block, everyone, axis=0, tiled=True)
+    kv_own, kv_far = key_sums(kv_sums)
+    dkv, key_terms = keys_back(kv_own, kv_far, raw, cosine, sine, head_gains, dlogit)
+    grad_o = tie(grad_o, dkv)
+    grad_o = grad_o + lax.ppermute(grad_o.astype(BF16), ("h", "m"), [(2, 1)]).astype(F32)
+    head_terms = jnp.concatenate([query_terms, key_terms], axis=0)
+    grad_q, grad_kv = tn(dq, normed), tn(dkv, normed)
+    query_part = grad_q.reshape(n, 2, small_block, width)
     second_part = jnp.concatenate(
         [
             jnp.transpose(query_part, (1, 0, 2, 3)).reshape(q_rows, width),
-            grad_in[q_rows : q_rows + 2 * kv_rows],
+            grad_kv[: 2 * kv_rows],
         ],
         axis=0,
     ).astype(BF16)
-    dnormed = sum_near(sum_core(nn(dall, w_in)))
+    dn_core = sum_core(nn(dq, w_in[:q_rows]) + nn(dkv, w_in[q_rows:]))
+    dnormed = sum_near(dn_core)
     norm_terms_in = jnp.sum(dnormed * y1, axis=0)
     grad_rows = dmiddle + norm_back(dnormed, y1, r1, norm_gains[0])
     if quarter > 1:
         second_part = second_part.reshape(4, quarter, -1, width)
         second_part = lax.psum_scatter(second_part, "i", scatter_dimension=1, tiled=True)
     second_part = second_part.reshape(4, 4 * small_block, width)
-    first_mid = turned(trade(first_grad, ("c", "x")))
     chunks = [
         lax.dynamic_index_in_dim(second_part, my_plane ^ k, 0, keepdims=False) for k in range(4)
     ]
     mine = chunks[0].astype(F32)
     for k, axes in ((1, ("m",)), (2, ("h",)), (3, ("h", "m"))):
         mine = mine + flip(chunks[k], *axes).astype(F32)
-    mine = tie(mine.astype(BF16), first_mid, old_rows)
+    mine = tie(mine.astype(BF16), dn_core)
+    mine_sum = mine
     pair = flip(mine, "m")
     mine, pair = (v.reshape(4, small_block, width) for v in (mine, pair))
     second_grad = jnp.concatenate(
@@ -855,13 +928,14 @@
     second_grad = jnp.where(
         my_plane == OUT, grad_o.astype(BF16).reshape(4, out_block, width), second_grad
     )
-    second_block = to_block(blend(second_old, second_grad))
-    small_z = sum_flips(
+    second_mid = turned(trade(second_grad, ("c", "x")))
+    second_block = blend(second_old, second_mid).reshape(4 * out_block, width)
+    small_z = (
         jnp.concatenate(
             [
                 lax.dynamic_update_slice_in_dim(
                     jnp.zeros((gate_head.shape[0], width), F32),
-                    grad_in[q_rows + 2 * kv_rows : q_rows + 2 * kv_rows + heads_here],
+                    grad_kv[2 * kv_rows : 2 * kv_rows + heads_here],
                     (my_x * 4 + sub) * heads_here,
                     0,
                 ),
@@ -870,32 +944,46 @@
                 jnp.pad(head_terms.reshape(1, 2 * head_dim), ((0, 0), (0, width - 2 * head_dim))),
             ],
             axis=0,
-        ),
-        (("m",), ("h",), ("h", "m")),
-    )
+        )
+    )
+    small = sum_flips(small_z, (("m",), ("h",), ("h", "m")))
     if quarter > 1:
-        small_z = lax.psum(small_z, "i")
-    second_near = gather_near(second_block)
-    output = swap_halves(tie(out_rows.astype(BF16), dall), my_h, my_x)
+        small = lax.psum(small, "i")
+    small = sum_flips(small, NEAR)
+    output = swap_halves(tie(out_rows.astype(BF16), mine_sum), my_h, my_x)
+    second_block = tie(second_block, small, output)
+    second_start = lax.all_gather(second_block, everyone, axis=0, tiled=True)
+    spot = me % (4 * n)
+    mine_now, other_now = owned_rows(
+        jnp.stack([spot, spot ^ 1]).reshape(1, 2),
+        (w_query, w_keyval, w_outproj, w_gateup, w_down),
+        n,
+        second_block,
+    )
     first_g = trade(tie(first_mid, second_block), ("h", "m"))
     if quarter > 1:
         first_g = lax.ppermute(first_g, ("i", "b"), fold_pairs(quarter))
     first_ortho = orthogonal(
-        [first_start], firsts(ff_block, False), 4 * ff_block, second_block
-    )
-    second_ortho = orthogonal(
-        pieces_far([tie(v, first_ortho) for v in second_near]), firsts(out_block, True), 4 * out_block, first_ortho
-    )
-    first_x = trade(first_ortho.reshape(4, ff_block, width), ("h", "m"))
-    second_ortho = tie(second_ortho, first_x, first_g)
+        [first_start], (mine_at * (4 * ff_block)).reshape(1, 1), 4 * ff_block, other_now
+    )
+    second_ortho = orthogonal([second_start], (mine_at * (4 * out_block)).reshape(1, 1), 4 * out_block, first_ortho)
+    sent = lax.ppermute(tie(grad_rows.astype(BF16), other_now), ("h", "x"), [(1, 2), (2, 1)])
+    grad_input = jnp.where(my_h == my_x, grad_rows, sent.astype(F32))
+    returned = jnp.concatenate(
+        [first_ortho.reshape(4, ff_block, width), tie(second_mid, first_ortho)], axis=1
+    )
+    returned = trade(tie(returned, first_g, sent), ("h", "m"))
+    if quarter > 1:
+        returned = lax.ppermute(returned, ("i", "b"), fold_pairs(quarter))
+    first_x, second_g = returned[:, :ff_block], returned[:, ff_block:]
+    old_rows = jnp.where(my_x == my_h, mine_now, flip(tie(other_now, first_ortho), "x"))
+    second_ortho = tie(second_ortho, returned, old_rows)
     second_x = trade(second_ortho.reshape(4, out_block, width), ("h", "m"))
-    second_g = to_owner(tie(second_grad, first_ortho), quarter, second_ortho)
-
-
-    grad_input = swap_halves(tie(grad_rows, first_ortho), my_h, my_x)
+    if quarter > 1:
+        second_x = lax.ppermute(second_x, ("i", "b"), fold_pairs(quarter))
+
 
     head_count = gate_head.shape[0]
-    small = sum_flips(tie(small_z, first_ortho), NEAR)
     small = sum_flips(tie(small, second_ortho), (("c",),))
     grad_gate = small[:head_count]
     grad_norm = small[head_count : head_count + 2]

time: 596 us -> 511 us (0.86)
  waiting for transfers between devices: 141 us -> 104 us
  other arithmetic: 78.4 us -> 49.4 us
  local copies, waits for them, and re-layouts: 67.2 us -> 46.5 us
  starting transfers between devices: 140 us -> 121 us
  blocking collectives: 0 us -> 15.1 us
  Pallas kernels: 116 us -> 128 us
    all_to_all x10 -> x5, waiting for transfers between devices: 44.1 us -> 11.3 us  [trade(): return lax.all_to_all(v, axes, split_axis=0, concat_axis=0, tiled=True)]
    all_to_all x10 -> x5, starting transfers between devices: 44.9 us -> 28.4 us  [trade(): return lax.all_to_all(v, axes, split_axis=0, concat_axis=0, tiled=True)]
    all_to_all x0 -> x1, blocking collectives: none -> 15.1 us  [trade(): return lax.all_to_all(v, axes, split_axis=0, concat_axis=0, tiled=True)]
    pallas_call x2 -> x5, Pallas kernels: 24.8 us -> 38.5 us  [the longest x1 18.4 us: attend_back(): pl.pallas_call(functools.partial(attend_back_kernel, scale, count), out_s...]
    dot_general x2 -> x0, local copies, waits for them, and re-layouts: 6.75 us -> none  [nt(): lax.dot_general(p, q, (((1,), (1,)), ((), ())), preferred_element_type=F32)]
    ppermute x2 -> x3, waiting for transfers between devices: 6.57 us -> 0.01 us  [the longest x1 0.01 us: on_device(): lax.ppermute(grad_o, ('h', 'm'), [(0, 1), (3, 2)]).astype(F32)]
    unnamed x183 -> x225, local copies, waits for them, and re-layouts: 32 us -> 35.8 us
    ppermute x67 -> x58, starting transfers between devices: 87.1 us -> 84.8 us  [flip(): lax.ppermute(v, tuple(sorted(axes, key=ALL.index)), [(j, j ^ last) for j...]
  transfers between devices with their start and end apart: 85 -> 72, of which waited for: 30 -> 24; matrix products, arithmetic and copies ran while one was open for 20% -> 13% of each run, Pallas kernels for 18% -> 24%
where the time goes in v2:
time: 511 us; the launch traced here: 501 us
  Pallas kernels  128 us (25%)
  starting transfers between devices  121 us (24%)
  waiting for transfers between devices  104 us (20%)
  other arithmetic  49.4 us (10%)
  local copies, waits for them, and re-layouts  46.5 us (9%)
  matrix products  21.6 us (4%)
  between operations  15.7 us (3%)
  blocking collectives  15.1 us (3%)
    ppermute x58, waiting for transfers between devices, flip(): lax.ppermute(v, tuple(sorted(axes, key=ALL.index)), [(j, j ^ last) for j...  92.9 us
    ppermute x58, starting transfers between devices, flip(): lax.ppermute(v, tuple(sorted(axes, key=ALL.index)), [(j, j ^ last) for j...  84.8 us
    pallas_call x2, Pallas kernels, orthogonal(): pl.pallas_call(functools.partial(schulz_kernel, count), out_shape=jax.Sha...  72 us
    unnamed x225, local copies, waits for them, and re-layouts  35.8 us
    all_to_all x5, starting transfers between devices, trade(): return lax.all_to_all(v, axes, split_axis=0, concat_axis=0, tiled=True)  28.4 us
    pallas_call x1, Pallas kernels, attend_back(): pl.pallas_call(functools.partial(attend_back_kernel, scale, count), out_s...  18.4 us
    all_to_all x1, blocking collectives, trade(): return lax.all_to_all(v, axes, split_axis=0, concat_axis=0, tiled=True)  15.1 us
    pallas_call x1, Pallas kernels, attend(): pl.pallas_call(without_tokens, out_shape=[shape_of(F32, heads, rows, dim)...  11.7 us
  transfers between devices with their start and end apart: 72, of which 24 were waited for; matrix products, arithmetic and copies ran while one was open for 13% of the time, Pallas kernels for 24%

profile of v2, /device:TPU:0, one launch (start us, length us, event | category | flops | bytes accessed | tf_op | source)
XLA Modules:
  0.0 501.4 jit_solution(2365931821133751019)
XLA Ops:
  20.1 8.7 %collective-permute-start.1 = (bf16[128,1024]{1,0:T(8,128)(2,1)}, bf16[128,1024]{1,0:T(8,128)(2,1)S(1)}, u32[]{:S(2)}, u32[]{:S(2)}) collective-permute-start(bf16[128,1024]{1,0:T(8,128)(2,1)} %tie.19.refs_0_), channel_id=1, source_target_pairs={{0,1},{1,0},{2,3},{3,2},{4,5},{5,4},{6,7},{7,6},{8,9},{9,8},{10,11... | collective-permute-start | bytes 786440 | tf_op jit(solution)/shard_map/ppermute | solution.py:39
  30.4 5.9 %collective-permute-done.1.refs_1_ = bf16[128,1024]{1,0:T(8,128)(2,1)S(1)} collective-permute-done((bf16[128,1024]{1,0:T(8,128)(2,1)}, bf16[128,1024]{1,0:T(8,128)(2,1)S(1)}, u32[]{:S(2)}, u32[]{:S(2)}) %collective-permute-start.1) | collective-permute-done | bytes 262176 | tf_op jit(solution)/shard_map/ppermute | solution.py:39
  36.3 5.3 %collective-permute-done.2.refs_2_ = bf16[128,1024]{1,0:T(8,128)(2,1)S(1)} collective-permute-done((bf16[128,1024]{1,0:T(8,128)(2,1)}, bf16[128,1024]{1,0:T(8,128)(2,1)S(1)}, u32[]{:S(2)}, u32[]{:S(2)}) %collective-permute-start.2) | collective-permute-done | bytes 262176 | tf_op jit(solution)/shard_map/ppermute | solution.py:39
  57.0 14.9 %collective-permute-start.10 = (bf16[128,1024]{1,0:T(8,128)(2,1)}, bf16[128,1024]{1,0:T(8,128)(2,1)}, u32[]{:S(2)}, u32[]{:S(2)}) collective-permute-start(bf16[128,1024]{1,0:T(8,128)(2,1)} %tie.20.refs_1_.refs_0_), channel_id=1, source_target_pairs={{0,1},{1,0},{2,3},{3,2},{4,5},{5,4},{6,7},{7,6},{8,9},{9,8},{10,11... | collective-permute-start | bytes 786440 | tf_op jit(solution)/shard_map/ppermute | solution.py:39
  77.5 11.7 %attend.1 = (f32[2,1024,128]{2,1,0:T(8,128)S(1)}, f32[2,1024,1]{2,1,0:T(8,128)S(1)}, bf16[1024,256]{1,0:T(8,128)(2,1)S(1)}) custom-call(bf16[2,1024,128]{2,1,0:T(8,128)(2,1)S(1)} %copy-done.35, f32[1024,128]{1,0:T(8,128)S(1)} %copy-done.67, s32[1024,1]{1,0:T(8,128)S(1)} %copy-done.51, s32[1,2048]{1,0:T(1,128)S(1)} %bitcast.73, ...), custom_call_target="tpu_custom_call" | custom-call | flops 13799999488 | bytes 1048576 | tf_op jit(solution)/shard_map/attend/pallas_call | solution.py:425
  104.4 7.5 %all-to-all-start = ((bf16[4,160,1024]{2,1,0:T(8,128)(2,1)}), bf16[4,160,1024]{2,1,0:T(8,128)(2,1)}, u32[]{:S(2)}, u32[]{:S(2)}) async-start(bf16[4,160,1024]{2,1,0:T(8,128)(2,1)} %copy-done.14), calls=%async_computation | async-start | bytes 2621440 | tf_op jit(solution)/shard_map/all_to_all | solution.py:115
  121.5 5.2 %collective-permute-done.17.refs_1_ = bf16[128,1024]{1,0:T(8,128)(2,1)S(1)} collective-permute-done((bf16[128,1024]{1,0:T(8,128)(2,1)S(1)}, bf16[128,1024]{1,0:T(8,128)(2,1)S(1)}, u32[]{:S(2)}, u32[]{:S(2)}) %collective-permute-start.17) | collective-permute-done | bytes 262176 | tf_op jit(solution)/shard_map/ppermute | solution.py:39
  126.7 4.4 collective-permute-done.18.refs_2_
  169.2 5.3 %collective-permute-done.32 = bf16[128,1024]{1,0:T(8,128)(2,1)S(1)} collective-permute-done((bf16[128,1024]{1,0:T(8,128)(2,1)S(1)}, bf16[128,1024]{1,0:T(8,128)(2,1)S(1)}, u32[]{:S(2)}, u32[]{:S(2)}) %collective-permute-start.32) | collective-permute-done | bytes 262176 | tf_op jit(solution)/shard_map/ppermute | solution.py:39
  180.0 6.0 %collective-permute-done.33.refs_1_ = bf16[128,1024]{1,0:T(8,128)(2,1)} collective-permute-done((bf16[128,1024]{1,0:T(8,128)(2,1)}, bf16[128,1024]{1,0:T(8,128)(2,1)}, u32[]{:S(2)}, u32[]{:S(2)}) %collective-permute-start.33) | collective-permute-done | bytes 262176 | tf_op jit(solution)/shard_map/ppermute | solution.py:39
  186.6 4.4 collective-permute-done.35.refs_3_
  199.2 18.4 %attend_back.1 = (bf16[1024,256]{1,0:T(8,128)(2,1)S(1)}, f32[1,128]{1,0:T(1,128)S(1)}, f32[2,1024,128]{2,1,0:T(8,128)S(1)}, bf16[2,1024,128]{2,1,0:T(8,128)(2,1)}) custom-call(bf16[2,1024,128]{2,1,0:T(8,128)(2,1)S(1)} %copy-done.37, bf16[2,1024,256]{2,1,0:T(8,128)(2,1)S(1)} %get-tuple-element.72.refs_1_.bw_ref, f32[3,1024,128]{2,1,0:T(8,128)S(1)} %copy-done.58, ...), custom_call_target="tpu_custom_call" | custom-call | flops 20700000256 | bytes 1048576 | tf_op jit(solution)/shard_map/attend_back/pallas_call | solution.py:522
  220.4 15.1 %all_to_all.30 = bf16[4,96,1024]{2,1,0:T(8,128)(2,1)S(1)} all-to-all(bf16[4,96,1024]{2,1,0:T(8,128)(2,1)} %tie.31), channel_id=1, replica_groups=mesh['h'=2,'m'=2,'i'=1,'b'=2,'c'=2,'x'=2] {'c','x'}, dimensions={0} | all-to-all | bytes 1572864 | tf_op jit(solution)/shard_map/all_to_all | solution.py:115
  253.7 7.1 %collective-permute-done.42 = bf16[128,1024]{1,0:T(8,128)(2,1)S(1)} collective-permute-done((bf16[128,1024]{1,0:T(8,128)(2,1)S(1)}, bf16[128,1024]{1,0:T(8,128)(2,1)S(1)}, u32[]{:S(2)}, u32[]{:S(2)}) %collective-permute-start.42) | collective-permute-done | bytes 262176 | tf_op jit(solution)/shard_map/ppermute | solution.py:39
  292.0 23.7 %collective-permute-done.45 = bf16[128,1024]{1,0:T(8,128)(2,1)S(1)} collective-permute-done((bf16[128,1024]{1,0:T(8,128)(2,1)S(1)}, bf16[128,1024]{1,0:T(8,128)(2,1)S(1)}, u32[]{:S(2)}, u32[]{:S(2)}) %collective-permute-start.45) | collective-permute-done | bytes 262176 | tf_op jit(solution)/shard_map/ppermute | solution.py:39
  324.6 4.6 collective-permute-start.54
  334.7 7.5 %collective-permute-start.55 = (f32[19,1024]{1,0:T(8,128)S(1)}, f32[19,1024]{1,0:T(8,128)S(1)}, u32[]{:S(2)}, u32[]{:S(2)}) collective-permute-start(f32[19,1024]{1,0:T(8,128)S(1)} %select_maximum_fusion), channel_id=1, source_target_pairs={{0,8},{8,0},{1,9},{9,1},{2,10},{10,2},{3,11},{11,3},{4,12},{12,4},... | collective-permute-start | bytes 233480 | tf_op jit(solution)/shard_map/ppermute | solution.py:39
  356.6 6.8 %collective-permute-done.58 = f32[19,1024]{1,0:T(8,128)S(1)} collective-permute-done((f32[19,1024]{1,0:T(8,128)S(1)}, f32[19,1024]{1,0:T(8,128)S(1)}, u32[]{:S(2)}, u32[]{:S(2)}) %collective-permute-start.58) | collective-permute-done | bytes 77856 | tf_op jit(solution)/shard_map/ppermute | solution.py:39
  375.6 6.0 %all-to-all-start.3 = ((bf16[4,96,1024]{2,1,0:T(8,128)(2,1)}), bf16[4,96,1024]{2,1,0:T(8,128)(2,1)S(1)}, u32[]{:S(2)}, u32[]{:S(2)}) async-start(bf16[4,96,1024]{2,1,0:T(8,128)(2,1)} %tie.33), calls=%async_computation.4 | async-start | bytes 1572864 | tf_op jit(solution)/shard_map/all_to_all | solution.py:115
  381.6 39.5 %schulz.2.refs_1_ = bf16[384,1024]{1,0:T(8,128)(2,1)S(1)} custom-call(s32[1,1]{1,0:T(1,128)} %bitcast.31.start_ref, bf16[3072,1024]{1,0:T(8,128)(2,1)} %all-gather.5.cloned.1.call-done.refs_0_, bf16[480,1024]{1,0:T(8,128)(2,1)S(1)} %copy-done.25), custom_call_target="tpu_custom_call" | custom-call | flops 47244640256 | bytes 12582912 | tf_op jit(solution)/shard_map/schulz/pallas_call | solution.py:680
  427.0 5.4 %all-to-all-start.4 = ((bf16[4,160,1024]{2,1,0:T(8,128)(2,1)}), bf16[4,160,1024]{2,1,0:T(8,128)(2,1)}, u32[]{:S(2)}, u32[]{:S(2)}) async-start(bf16[4,160,1024]{2,1,0:T(8,128)(2,1)} %tie.34), calls=%async_computation.5 | async-start | bytes 2621440 | tf_op jit(solution)/shard_map/all_to_all | solution.py:115
  434.5 32.5 %schulz.3.refs_0_ = bf16[256,1024]{1,0:T(8,128)(2,1)} custom-call(s32[1,1]{1,0:T(1,128)} %bitcast.30.start_ref, bf16[2048,1024]{1,0:T(8,128)(2,1)S(1)} %copy-done.56, bf16[384,1024]{1,0:T(8,128)(2,1)S(1)} %copy-done.13), custom_call_target="tpu_custom_call" | custom-call | flops 47244640256 | bytes 8388608 | tf_op jit(solution)/shard_map/schulz/pallas_call | solution.py:680
  474.1 5.2 %all-to-all-start.5 = ((bf16[4,64,1024]{2,1,0:T(8,128)(2,1)}), bf16[4,64,1024]{2,1,0:T(8,128)(2,1)S(1)}, u32[]{:S(2)}, u32[]{:S(2)}) async-start(bf16[4,64,1024]{2,1,0:T(8,128)(2,1)} %bitcast.36), calls=%async_computation.6 | async-start | bytes 1048576 | tf_op jit(solution)/shard_map/all_to_all | solution.py:115
  484.7 8.7 %all-to-all-done.5.items = bf16[4,64,1024]{2,1,0:T(8,128)(2,1)S(1)} async-done(((bf16[4,64,1024]{2,1,0:T(8,128)(2,1)}), bf16[4,64,1024]{2,1,0:T(8,128)(2,1)S(1)}, u32[]{:S(2)}, u32[]{:S(2)}) %all-to-all-start.5) | async-done | bytes 524320 | tf_op jit(solution)/shard_map/all_to_all | solution.py:115
  (490 shorter events, 225.6 us)
Async XLA Ops:
  50.4 23.1 %collective-permute-start.8 = (bf16[2,1024,128]{2,1,0:T(8,128)(2,1)}, bf16[2,1024,128]{2,1,0:T(8,128)(2,1)}, u32[]{:S(2)}, u32[]{:S(2)}) collective-permute-start(bf16[2,1024,128]{2,1,0:T(8,128)(2,1)} %get-tuple-element.65.refs_4_.refs_0_), channel_id=1, source_target_pairs={{0,8},{8,0},{1,9},{9,1},{2,10},{10,2},{3,11},{11,3},{4,12},{12,4},... | collective-permute-start | bytes 1572872 | tf_op jit(solution)/shard_map/ppermute | solution.py:39
  57.0 35.0 %collective-permute-start.10 = (bf16[128,1024]{1,0:T(8,128)(2,1)}, bf16[128,1024]{1,0:T(8,128)(2,1)}, u32[]{:S(2)}, u32[]{:S(2)}) collective-permute-start(bf16[128,1024]{1,0:T(8,128)(2,1)} %tie.20.refs_1_.refs_0_), channel_id=1, source_target_pairs={{0,1},{1,0},{2,3},{3,2},{4,5},{5,4},{6,7},{7,6},{8,9},{9,8},{10,11... | collective-permute-start | bytes 786440 | tf_op jit(solution)/shard_map/ppermute | solution.py:39
  72.0 20.1 %collective-permute-start.11 = (bf16[128,1024]{1,0:T(8,128)(2,1)}, bf16[128,1024]{1,0:T(8,128)(2,1)}, u32[]{:S(2)}, u32[]{:S(2)}) collective-permute-start(bf16[128,1024]{1,0:T(8,128)(2,1)} %tie.20.refs_1_.refs_0_), channel_id=1, source_target_pairs={{0,4},{4,0},{1,5},{5,1},{2,6},{6,2},{3,7},{7,3},{8,12},{12,8},{9,1... | collective-permute-start | bytes 786440 | tf_op jit(solution)/shard_map/ppermute | solution.py:39
  73.0 19.1 %collective-permute-start.12 = (bf16[128,1024]{1,0:T(8,128)(2,1)}, bf16[128,1024]{1,0:T(8,128)(2,1)}, u32[]{:S(2)}, u32[]{:S(2)}) collective-permute-start(bf16[128,1024]{1,0:T(8,128)(2,1)} %tie.20.refs_1_.refs_0_), channel_id=1, source_target_pairs={{0,5},{1,4},{4,1},{5,0},{2,7},{3,6},{6,3},{7,2},{8,13},{9,12},{12,... | collective-permute-start | bytes 786440 | tf_op jit(solution)/shard_map/ppermute | solution.py:39
  104.4 39.6 %all-to-all-start = ((bf16[4,160,1024]{2,1,0:T(8,128)(2,1)}), bf16[4,160,1024]{2,1,0:T(8,128)(2,1)}, u32[]{:S(2)}, u32[]{:S(2)}) async-start(bf16[4,160,1024]{2,1,0:T(8,128)(2,1)} %copy-done.14), calls=%async_computation | async-start | bytes 2621440 | tf_op jit(solution)/shard_map/all_to_all | solution.py:115
  111.8 108.6 %reduce-scatter.2.cloned.1.call-start = ((), (), s32[]{:S(2)}) async-start(), calls=%async_computation.8 | async-start | bytes 3932160 | tf_op jit(solution)/shard_map/reduce_scatter | solution.py:851
  152.1 229.6 %all-gather.5.cloned.1.call-start = ((), (), s32[]{:S(2)}) async-start(), calls=%async_computation.9 | async-start | bytes 7077888 | tf_op jit(solution)/shard_map/all_gather | solution.py:892
  241.8 19.0 %collective-permute-start.42 = (bf16[128,1024]{1,0:T(8,128)(2,1)S(1)}, bf16[128,1024]{1,0:T(8,128)(2,1)S(1)}, u32[]{:S(2)}, u32[]{:S(2)}) collective-permute-start(bf16[128,1024]{1,0:T(8,128)(2,1)S(1)} %get-tuple-element.134), channel_id=1, source_target_pairs={{0,5},{1,4},{4,1},{5,0},{2,7},{3,6},{6,3},{7,2},{8,13},{9,12},{12,... | collective-permute-start | bytes 786440 | tf_op jit(solution)/shard_map/ppermute | solution.py:39
  244.2 18.7 %collective-permute-start.43 = (bf16[2,1024,128]{2,1,0:T(8,128)(2,1)}, bf16[2,1024,128]{2,1,0:T(8,128)(2,1)}, u32[]{:S(2)}, u32[]{:S(2)}) collective-permute-start(bf16[2,1024,128]{2,1,0:T(8,128)(2,1)} %get-tuple-element.76), channel_id=1, source_target_pairs={{0,8},{8,0},{1,9},{9,1},{2,10},{10,2},{3,11},{11,3},{4,12},{12,4},... | collective-permute-start | bytes 1572872 | tf_op jit(solution)/shard_map/ppermute | solution.py:39
  249.0 25.1 %collective-permute-start.52 = (bf16[256,1024]{1,0:T(8,128)(2,1)}, bf16[256,1024]{1,0:T(8,128)(2,1)}, u32[]{:S(2)}, u32[]{:S(2)}) collective-permute-start(bf16[256,1024]{1,0:T(8,128)(2,1)} %convolution_convert_fusion.2), channel_id=1, source_target_pairs={{0,8},{24,16},{1,9},{25,17},{2,10},{26,18},{3,11},{27,19},{4,12},{... | collective-permute-start | bytes 1572872 | tf_op jit(solution)/shard_map/ppermute | solution.py:880
  274.1 42.4 %collective-permute-start.47 = (bf16[512,1024]{1,0:T(8,128)(2,1)}, bf16[512,1024]{1,0:T(8,128)(2,1)}, u32[]{:S(2)}, u32[]{:S(2)}) collective-permute-start(bf16[512,1024]{1,0:T(8,128)(2,1)} %slice.286), channel_id=1, source_target_pairs={{0,2},{2,0},{1,3},{3,1},{4,6},{6,4},{5,7},{7,5},{8,10},{10,8},{9,1... | collective-permute-start | bytes 3145736 | tf_op jit(solution)/shard_map/ppermute | solution.py:39
  279.2 45.2 %collective-permute-start.53 = (bf16[256,1024]{1,0:T(8,128)(2,1)S(1)}, bf16[256,1024]{1,0:T(8,128)(2,1)S(1)}, u32[]{:S(2)}, u32[]{:S(2)}) collective-permute-start(bf16[256,1024]{1,0:T(8,128)(2,1)S(1)} %convert_element_type.218), channel_id=1, source_target_pairs={{16,8},{17,9},{18,10},{19,11},{20,12},{21,13},{22,14},{23,15}} | collective-permute-start | bytes 1572872 | tf_op jit(solution)/shard_map/ppermute | solution.py:896
  285.2 30.4 %collective-permute-start.45 = (bf16[128,1024]{1,0:T(8,128)(2,1)S(1)}, bf16[128,1024]{1,0:T(8,128)(2,1)S(1)}, u32[]{:S(2)}, u32[]{:S(2)}) collective-permute-start(bf16[128,1024]{1,0:T(8,128)(2,1)S(1)} %get-tuple-element.132), channel_id=1, source_target_pairs={{0,16},{16,0},{1,17},{17,1},{2,18},{18,2},{3,19},{19,3},{4,20},{20... | collective-permute-start | bytes 786440 | tf_op jit(solution)/shard_map/ppermute | solution.py:39
  287.4 28.2 %collective-permute-start.46 = (bf16[128,1024]{1,0:T(8,128)(2,1)S(1)}, bf16[128,1024]{1,0:T(8,128)(2,1)S(1)}, u32[]{:S(2)}, u32[]{:S(2)}) collective-permute-start(bf16[128,1024]{1,0:T(8,128)(2,1)S(1)} %get-tuple-element.131), channel_id=1, source_target_pairs={{0,24},{8,16},{16,8},{24,0},{1,25},{9,17},{17,9},{25,1},{2,26},{10... | collective-permute-start | bytes 786440 | tf_op jit(solution)/shard_map/ppermute | solution.py:39
  324.6 21.9 %collective-permute-start.54 = (bf16[128,1024]{1,0:T(8,128)(2,1)}, bf16[128,1024]{1,0:T(8,128)(2,1)S(1)}, u32[]{:S(2)}, u32[]{:S(2)}) collective-permute-start(bf16[128,1024]{1,0:T(8,128)(2,1)} %tie.26.refs_1_), channel_id=1, source_target_pairs={{0,8},{8,0},{1,9},{9,1},{2,10},{10,2},{3,11},{11,3},{4,12},{12,4},... | collective-permute-start | bytes 786440 | tf_op jit(solution)/shard_map/ppermute | solution.py:39
  329.2 26.7 %collective-permute-start.48 = (bf16[128,1024]{1,0:T(8,128)(2,1)}, bf16[128,1024]{1,0:T(8,128)(2,1)S(1)}, u32[]{:S(2)}, u32[]{:S(2)}) collective-permute-start(bf16[128,1024]{1,0:T(8,128)(2,1)} %tie.27), channel_id=1, source_target_pairs={{1,16},{16,1},{3,18},{18,3},{5,20},{20,5},{7,22},{22,7},{9,24},{24... | collective-permute-start | bytes 786440 | tf_op jit(solution)/shard_map/ppermute | solution.py:107
  334.7 17.1 %collective-permute-start.55 = (f32[19,1024]{1,0:T(8,128)S(1)}, f32[19,1024]{1,0:T(8,128)S(1)}, u32[]{:S(2)}, u32[]{:S(2)}) collective-permute-start(f32[19,1024]{1,0:T(8,128)S(1)} %select_maximum_fusion), channel_id=1, source_target_pairs={{0,8},{8,0},{1,9},{9,1},{2,10},{10,2},{3,11},{11,3},{4,12},{12,4},... | collective-permute-start | bytes 233480 | tf_op jit(solution)/shard_map/ppermute | solution.py:39
  347.5 17.6 %all-to-all-start.1 = ((bf16[4,64,1024]{2,1,0:T(8,128)(2,1)}), bf16[4,64,1024]{2,1,0:T(8,128)(2,1)S(1)}, u32[]{:S(2)}, u32[]{:S(2)}) async-start(bf16[4,64,1024]{2,1,0:T(8,128)(2,1)} %maximum_select_fusion), calls=%async_computation.1 | async-start | bytes 1048576 | tf_op jit(solution)/shard_map/all_to_all | solution.py:115
  351.8 80.5 %all-gather.3.cloned.1.call-start = ((), (), s32[]{:S(2)}) async-start(), calls=%async_computation.7 | async-start | bytes 4718592 | tf_op jit(solution)/shard_map/all_gather | solution.py:955
  372.9 52.5 %collective-permute-start.61 = (bf16[128,1024]{1,0:T(8,128)(2,1)}, bf16[128,1024]{1,0:T(8,128)(2,1)S(1)}, u32[]{:S(2)}, u32[]{:S(2)}) collective-permute-start(bf16[128,1024]{1,0:T(8,128)(2,1)} %tie.30), channel_id=1, source_target_pairs={{1,16},{16,1},{3,18},{18,3},{5,20},{20,5},{7,22},{22,7},{9,24},{24... | collective-permute-start | bytes 786440 | tf_op jit(solution)/shard_map/ppermute | solution.py:970
  375.6 49.8 %all-to-all-start.3 = ((bf16[4,96,1024]{2,1,0:T(8,128)(2,1)}), bf16[4,96,1024]{2,1,0:T(8,128)(2,1)S(1)}, u32[]{:S(2)}, u32[]{:S(2)}) async-start(bf16[4,96,1024]{2,1,0:T(8,128)(2,1)} %tie.33), calls=%async_computation.4 | async-start | bytes 1572864 | tf_op jit(solution)/shard_map/all_to_all | solution.py:115
  422.0 45.1 %collective-permute-start.62 = (bf16[480,1024]{1,0:T(8,128)(2,1)}, bf16[480,1024]{1,0:T(8,128)(2,1)S(1)}, u32[]{:S(2)}, u32[]{:S(2)}) collective-permute-start(bf16[480,1024]{1,0:T(8,128)(2,1)} %tie.35), channel_id=1, source_target_pairs={{0,1},{1,0},{2,3},{3,2},{4,5},{5,4},{6,7},{7,6},{8,9},{9,8},{10,11... | collective-permute-start | bytes 2949128 | tf_op jit(solution)/shard_map/ppermute | solution.py:39
  427.0 41.3 %all-to-all-start.4 = ((bf16[4,160,1024]{2,1,0:T(8,128)(2,1)}), bf16[4,160,1024]{2,1,0:T(8,128)(2,1)}, u32[]{:S(2)}, u32[]{:S(2)}) async-start(bf16[4,160,1024]{2,1,0:T(8,128)(2,1)} %tie.34), calls=%async_computation.5 | async-start | bytes 2621440 | tf_op jit(solution)/shard_map/all_to_all | solution.py:115
  474.1 19.4 %all-to-all-start.5 = ((bf16[4,64,1024]{2,1,0:T(8,128)(2,1)}), bf16[4,64,1024]{2,1,0:T(8,128)(2,1)S(1)}, u32[]{:S(2)}, u32[]{:S(2)}) async-start(bf16[4,64,1024]{2,1,0:T(8,128)(2,1)} %bitcast.36), calls=%async_computation.6 | async-start | bytes 1048576 | tf_op jit(solution)/shard_map/all_to_all | solution.py:115
  (160 other events, 1039.9 us)
Sparse Core Ops, SparseCore 0:
  152.2 59.5 reduce-scatter.1
  238.7 50.5 all-gather.4
  367.5 39.8 all-gather.2
